TPU v7x, 256 devices: a whole 4x4x8 slice. The times are simulated.
256 devices in a mesh: dp: 8 (over z_hi, core), expert: 32 (over z_lo, y, x).
Axes of the slice: x: 4, y: 4, z: 8 (z_hi: 4, z_lo: 2; z = z_hi * 2 + z_lo), core: 2. Of those that a mesh axis runs over, the one named last changes fastest.
Arguments:
- out_cot: bfloat16 [32768, 4096], P(('dp', 'expert')), may hold values from -0.75 to 0.75
- route_ids: int32 [32768, 8], P(('dp', 'expert')), may hold values from 0 to 127, all different within a row; in each aligned block of 128 rows (0 to 127, 128 to 255, ...) at most 16 rows name the same one
- route_weight: float32 [32768, 8], P(('dp', 'expert')), may hold values from 0.05 to 0.4
- saved_gate: bfloat16 [8, 32, 512, 768], P('dp', 'expert'), may hold values from -6 to 6
- saved_up: bfloat16 [8, 32, 512, 768], P('dp', 'expert'), may hold values from -6 to 6
- down_weight: bfloat16 [32, 768, 4096], P('expert'), may hold values from -0.21875 to 0.21875
- moe_input: bfloat16 [32768, 4096], P(('dp', 'expert')), may hold values from -24 to 24
Outputs:
- gate_grad: bfloat16 [8, 32, 512, 768], P('dp', 'expert')
- up_grad: bfloat16 [8, 32, 512, 768], P('dp', 'expert')
- down_grad: float32 [32, 768, 4096], P('expert', 'dp')
- route_grad: float32 [32768, 8], P(('dp', 'expert'))
- router_grad: float32 [4096, 128], P(('dp', 'expert'))
Inputs may be any that keep to these rules, and one draw needn't show every extreme that they name: `route_ids`: each row names 8 different experts; among the rows of one device (aligned blocks of 128 rows) no expert is named by more than 16 rows, a bound that some block reaches.
All inputs are finite; a program needn't handle non-finite values.
Results may differ from a plain program's by a relative error of at most 0.015.
Values may be sent and summed in bfloat16 or wider, within the bound.
A program may use at most 128 MiB of HBM per device.

v0:
```python
import jax
import jax.numpy as jnp
from jax import lax
from jax.sharding import PartitionSpec as P

EXP_DEV = 4


def per_device(out_cot, route_ids, route_weight, saved_gate, saved_up, down_weight, moe_input):
    n_expert = lax.axis_size("expert")
    slots = saved_gate.shape[2]
    most = slots // n_expert
    width = out_cot.shape[1]
    all_experts = EXP_DEV * n_expert
    hit = route_ids % EXP_DEV == 0
    target = route_ids // EXP_DEV
    targets = jnp.arange(n_expert, dtype=jnp.int32)
    select = hit[:, :, None] & (target[:, :, None] == targets[None, None, :])
    onehot = jnp.sum(select.astype(jnp.int32), 1)
    rank = jnp.cumsum(onehot, 0) - onehot
    places = jnp.arange(most, dtype=jnp.int32)
    placer = (onehot.T[:, None, :] == 1) & (rank.T[:, None, :] == places[None, :, None])
    placer_bf = placer.astype(jnp.bfloat16)
    placer_fl = placer.astype(jnp.float32)
    send_rows = jnp.einsum(
        "jrt,td->jrd", placer_bf, out_cot, preferred_element_type=jnp.float32
    ).astype(jnp.bfloat16)
    token_weight = jnp.sum(jnp.where(select, route_weight[:, :, None], 0.0), 1)
    send_weight = jnp.einsum(
        "jrt,tj->jr", placer_fl, token_weight, precision=lax.Precision.HIGHEST
    ).astype(jnp.bfloat16)
    recv_rows, recv_weight = (
        lax.all_to_all(send_rows, "expert", split_axis=0, concat_axis=0, tiled=True),
        lax.all_to_all(send_weight, "expert", split_axis=0, concat_axis=0, tiled=True),
    )
    rows = recv_rows.reshape(slots, width)
    slot_weight = recv_weight.reshape(slots)
    matrix = down_weight[0]
    gate = saved_gate[0, 0].astype(jnp.float32)
    upper = saved_up[0, 0].astype(jnp.float32)
    sigma = jax.nn.sigmoid(gate)
    active = gate * sigma
    hidden = (active * upper).astype(jnp.bfloat16)
    expert_out = jnp.dot(hidden, matrix, preferred_element_type=jnp.float32)
    slot_dot = jnp.sum(expert_out * rows.astype(jnp.float32), -1)
    back = lax.all_to_all(
        slot_dot.reshape(n_expert, most), "expert", split_axis=0, concat_axis=0, tiled=True
    )
    weighted = (slot_weight.astype(jnp.float32)[:, None] * rows.astype(jnp.float32)).astype(
        jnp.bfloat16
    )
    hidden_cot = lax.dot_general(
        weighted, matrix, (((1,), (1,)), ((), ())), preferred_element_type=jnp.float32
    )
    up_grad = (hidden_cot * active).astype(jnp.bfloat16)
    gate_grad = (hidden_cot * upper * sigma * (1.0 + gate * (1.0 - sigma))).astype(jnp.bfloat16)
    piece = hidden
    down_part = lax.psum_scatter(
        lax.dot_general(
            piece, weighted, (((0,), (0,)), ((), ())), preferred_element_type=jnp.float32
        ).astype(jnp.bfloat16),
        "dp",
        scatter_dimension=0,
        tiled=True,
    ).astype(jnp.float32)
    token_dot = jnp.einsum("jrt,jr->tj", placer_fl, back, precision=lax.Precision.HIGHEST)
    route_grad = jnp.sum(jnp.where(select, token_dot[:, None, :], 0.0), -1)
    mixed = jnp.sum(route_weight * route_grad, -1, keepdims=True)
    per_pick = route_weight * (route_grad - mixed)
    columns = jnp.arange(all_experts, dtype=jnp.int32)
    matches = route_ids[:, :, None] == columns[None, None, :]
    logit_cot = jnp.sum(jnp.where(matches, per_pick[:, :, None], 0.0), 1).astype(jnp.bfloat16)
    piece = moe_input
    product = lax.dot_general(
        piece, logit_cot, (((0,), (0,)), ((), ())), preferred_element_type=jnp.float32
    )
    router_part = lax.psum_scatter(
        0.015625 * product, ("dp", "expert"), scatter_dimension=0, tiled=True
    )
    return (gate_grad[None, None], up_grad[None, None], down_part[None], route_grad, router_part)


def solution(mesh):
    placed = (
        P(("dp", "expert"), None),
        P(("dp", "expert"), None),
        P(("dp", "expert"), None),
        P("dp", "expert", None, None),
        P("dp", "expert", None, None),
        P("expert", None, None),
        P(("dp", "expert"), None),
    )
    return jax.shard_map(
        per_device,
        mesh=mesh,
        in_specs=placed,
        out_specs=(
            P("dp", "expert", None, None),
            P("dp", "expert", None, None),
            P("expert", "dp", None),
            P(("dp", "expert"), None),
            P(("dp", "expert"), None),
        ),
        check_vma=False,
    )
```

profile of v0, /device:TPU:0, one launch (start us, length us, event | category | flops | bytes accessed | tf_op | source)
XLA Modules:
  0.0 1472.7 jit_solution(250406479674331236)
XLA Ops:
  7.2 0.8 add_select_fusion
  8.0 0.7 fusion.42
  8.7 0.1 copy.47
  8.8 0.2 reduce_window_sum.11
  9.0 0.1 copy.49
  9.1 1.3 convolution_convert_fusion.1
  10.4 57.2 %all_to_all.26 = bf16[32,16,4096]{2,1,0:T(8,128)(2,1)S(1)} all-to-all(bf16[32,16,4096]{2,1,0:T(8,128)(2,1)S(1)} %convolution_convert_fusion.1), channel_id=1, replica_groups=mesh['dp'=8,'expert'=32] {'expert'}, dimensions={0} | all-to-all | bytes 8388608 | tf_op jit(solution)/shard_map/all_to_all | solution.py:33
  67.6 1.9 copy-done.1
  69.6 4.2 fusion
  73.8 0.1 all_to_all.20
  73.9 13.2 all_to_all.27
  87.0 0.3 fusion.28
  87.4 0.3 fusion.31
  87.7 0.1 copy.56
  87.8 0.1 copy.50
  87.9 11.5 all_to_all.28
  99.5 3.7 multiply_convert_fusion
  103.2 2.0 copy-done.2
  105.3 5.6 convolution_convert_fusion
  110.9 0.2 reduce-scatter.7.cloned.1.call-start
  111.1 0.4 copy-done.5
  111.6 0.1 copy.52
  111.7 0.1 copy.53
  111.8 0.4 select_reduce_fusion
  112.2 1.7 fusion.4
  113.9 1.8 copy.59
  115.7 1.1 copy-done.7
  116.8 0.2 copy-done.9
  117.0 9.2 fusion.25
  126.3 58.4 %reduce-scatter.5.cloned.1.call-done = bf16[96,4096]{1,0:T(8,128)(2,1)} async-done(((bf16[768,4096]{1,0:T(8,128)(2,1)}), bf16[96,4096]{1,0:T(8,128)(2,1)}) %reduce-scatter.5.cloned.1.call-update) | async-done | bytes 786448 | tf_op jit(solution)/shard_map/reduce_scatter | solution.py:58
  184.7 2.4 bitcast_convert_fusion
  187.1 1278.8 %reduce-scatter.7.cloned.1.call-done = f32[16,128]{1,0:T(8,128)} async-done(((f32[4096,128]{1,0:T(8,128)}), f32[16,128]{1,0:T(8,128)}) %reduce-scatter.7.cloned.1.call-update) | async-done | bytes 8208
  (31 shorter events, 0.3 us)
Async XLA Ops:
  7.2 1.9 copy-start
  7.2 177.5 %reduce-scatter.5.cloned.1.call-start = ((), (), s32[]{:S(2)}) async-start(), calls=%async_computation.5 | async-start | bytes 7077888 | tf_op jit(solution)/shard_map/reduce_scatter | solution.py:58
  9.1 60.5 %slice-start = ((s8[6291456]{0:T(1024)(128)(4,1)}), s8[4194304]{0:T(1024)(128)(4,1)S(1)}, s32[]{:S(2)}) async-start(s8[6291456]{0:T(1024)(128)(4,1)} %bitcast.108), calls=%async_computation.7 | async-start | bytes 8388608
  10.4 59.2 %slice-start.1 = ((s8[6291456]{0:T(1024)(128)(4,1)}), s8[2097152]{0:T(1024)(128)(4,1)S(1)}, s32[]{:S(2)}) async-start(s8[6291456]{0:T(1024)(128)(4,1)} %bitcast.108), calls=%async_computation.8 | async-start | bytes 4194304
  10.4 59.2 %copy-start.6 = (bf16[1,1,512,768]{3,2,1,0:T(8,128)(2,1)S(1)}, bf16[1,1,512,768]{3,2,1,0:T(8,128)(2,1)}, u32[]{:S(2)}) copy-start(bf16[1,1,512,768]{3,2,1,0:T(8,128)(2,1)} %param.10) | copy-start | bytes 2359300
  10.4 59.2 %copy-start.8 = (bf16[1,1,512,768]{3,2,1,0:T(8,128)(2,1)S(1)}, bf16[1,1,512,768]{3,2,1,0:T(8,128)(2,1)}, u32[]{:S(2)}) copy-start(bf16[1,1,512,768]{3,2,1,0:T(8,128)(2,1)} %param.11) | copy-start | bytes 2359300
  67.6 1.9 copy-start.1
  69.6 17.7 %copy-start.3 = (f32[128,8]{0,1:T(8,128)S(1)}, f32[128,8]{0,1:T(8,128)}, u32[]{:S(2)}) copy-start(f32[128,8]{0,1:T(8,128)} %param.9) | copy-start | bytes 12292
  87.4 24.3 %copy-start.4 = (f32[128,8]{0,1:T(8,128)}, f32[128,8]{0,1:T(8,128)S(1)}, u32[]{:S(2)}) copy-start(f32[128,8]{0,1:T(8,128)S(1)} %get-tuple-element.30) | copy-start | bytes 12292
  103.2 2.0 copy-start.2
  110.9 0.7 copy-start.5
  110.9 1355.0 %reduce-scatter.7.cloned.1.call-start = ((), (), s32[]{:S(2)}) async-start(), calls=%async_computation.6 | async-start | bytes 2105344
  115.7 1.1 copy-start.7
  115.7 1.4 copy-start.9
Sparse Core Ops, SparseCore 0:
  111.0 73.5 reduce-scatter.4
  187.7 1278.0 reduce-scatter.6
where the time goes:
time: 1470 us
  waiting for transfers between devices  1340 us (91%)
  blocking collectives  81.9 us (6%)
  matrix products  22.6 us (2%)
    unnamed x3, waiting for transfers between devices  1280 us
    reduce_scatter x1, waiting for transfers between devices, per_device(): lax.psum_scatter(lax.dot_general(piece, weighted, (((0,), (0,)), ((), ())...  58.4 us
    all_to_all x1, blocking collectives, per_device(): lax.all_to_all(send_rows, 'expert', split_axis=0, concat_axis=0, tiled=True)  57.2 us
  transfers between devices with their start and end apart: 2, of which 2 were waited for; matrix products, arithmetic and copies ran while one was open for 1% of the time, Pallas kernels for 0%

commit v1 on v0

--- a/solution.py
+++ b/solution.py
@@ -74,9 +74,13 @@
     product = lax.dot_general(
         piece, logit_cot, (((0,), (0,)), ((), ())), preferred_element_type=jnp.float32
     )
-    router_part = lax.psum_scatter(
-        0.015625 * product, ("dp", "expert"), scatter_dimension=0, tiled=True
-    )
+    n_dp = lax.axis_size("dp")
+    own = product.shape[0] // (n_dp * n_expert)
+    blocks = (0.015625 * product).reshape(n_dp, n_expert, own, all_experts)
+    across = lax.all_to_all(blocks, "expert", split_axis=1, concat_axis=1, tiled=True)
+    partial = jnp.sum(across, 1)
+    along = lax.all_to_all(partial, "dp", split_axis=0, concat_axis=0, tiled=True)
+    router_part = jnp.sum(along, 0)
     return (gate_grad[None, None], up_grad[None, None], down_part[None], route_grad, router_part)
 
 

time: 1470 us -> 222 us (0.15)
  the two profiles are of different devices: /device:TPU:0 before, /device:TPU:1 now
where the time goes in v1:
time: 222 us; the launch traced here: 217 us
  blocking collectives  127 us (57%)
  matrix products  22.9 us (10%)
  starting transfers between devices  17.9 us (8%)
  waiting for transfers between devices  16.8 us (8%)
  between operations  14.2 us (6%)
  other arithmetic  9.64 us (4%)
  local copies, waits for them, and re-layouts  8.9 us (4%)
    all_to_all x1, blocking collectives, per_device(): lax.all_to_all(send_rows, 'expert', split_axis=0, concat_axis=0, tiled=True)  57.8 us
    all_to_all x1, blocking collectives, per_device(): lax.all_to_all(blocks, 'expert', split_axis=1, concat_axis=1, tiled=True)  45.7 us
    all_to_all x1, starting transfers between devices, per_device(): lax.all_to_all(partial, 'dp', split_axis=0, concat_axis=0, tiled=True)  17.8 us
    reduce_scatter x1, waiting for transfers between devices, per_device(): lax.psum_scatter(lax.dot_general(piece, weighted, (((0,), (0,)), ((), ())...  16.8 us
    all_to_all x1, blocking collectives, per_device(): lax.all_to_all(slot_dot.reshape(n_expert, most), 'expert', split_axis=0,...  13.6 us
    all_to_all x1, blocking collectives, per_device(): lax.all_to_all(send_weight, 'expert', split_axis=0, concat_axis=0, tiled=...  10.1 us
    dot_general x1, matrix products, per_device(): lax.dot_general(weighted, matrix, (((1,), (1,)), ((), ())), preferred_ele...  9.49 us
    dot_general x1, matrix products, per_device(): lax.dot_general(piece, weighted, (((0,), (0,)), ((), ())), preferred_elem...  5.62 us
  transfers between devices with their start and end apart: 2, of which 1 were waited for; matrix products, arithmetic and copies ran while one was open for 8% of the time, Pallas kernels for 0%

profile of v1, /device:TPU:1, one launch (start us, length us, event | category | flops | bytes accessed | tf_op | source)
XLA Modules:
  0.0 217.5 jit_solution(6800175111797317860)
XLA Ops:
  7.2 0.8 add_select_fusion
  8.0 0.7 fusion.42
  8.7 0.1 copy.48
  8.8 0.2 reduce_window_sum.11
  9.1 1.3 convolution_convert_fusion.1
  10.4 57.8 %all_to_all.36 = bf16[32,16,4096]{2,1,0:T(8,128)(2,1)S(1)} all-to-all(bf16[32,16,4096]{2,1,0:T(8,128)(2,1)S(1)} %convolution_convert_fusion.1), channel_id=1, replica_groups=mesh['dp'=8,'expert'=32] {'expert'}, dimensions={0} | all-to-all | bytes 8388608 | tf_op jit(solution)/shard_map/all_to_all | solution.py:33
  68.2 1.9 copy-done.1
  70.2 4.2 %fusion = f32[512]{0:T(512)S(1)} fusion(bf16[1,768,4096]{2,1,0:T(8,128)(2,1)S(1)} %bitcast.110, bf16[32,16,4096]{2,1,0:T(8,128)(2,1)S(1)} %all_to_all.36, bf16[1,1,512,768]{3,2,1,0:T(8,128)(2,1)S(1)} %copy-done.7, bf16[1,1,512,768]{3,2,1,0:T(8,128)(2,1)S(1)} %copy-done.6), kind=kOutput, calls=%fused_computation.1 | convolution fusion | flops 3230662144 | bytes 12060672 | tf_op jit(solution)/shard_map/dot_general | solution.py:44
  74.4 0.1 all_to_all.26
  74.4 13.6 %all_to_all.37 = f32[32,1,16]{2,1,0:T(1,128)S(1)} all-to-all(f32[32,1,16]{2,1,0:T(1,128)S(1)} %bitcast.106), channel_id=1, replica_groups=mesh['dp'=8,'expert'=32] {'expert'}, dimensions={0} | all-to-all | bytes 4096 | tf_op jit(solution)/shard_map/all_to_all | solution.py:46
  88.0 0.3 fusion.28
  88.4 0.3 fusion.31
  88.7 0.1 copy.58
  88.8 0.1 copy.51
  88.9 10.1 %all_to_all.38 = bf16[32,1,16]{2,1,0:T(2,128)(2,1)S(1)} all-to-all(bf16[32,1,16]{2,1,0:T(2,128)(2,1)S(1)} %copy.51), channel_id=1, replica_groups=mesh['dp'=8,'expert'=32] {'expert'}, dimensions={0} | all-to-all | bytes 2048 | tf_op jit(solution)/shard_map/all_to_all | solution.py:34
  99.1 3.7 %multiply_convert_fusion = bf16[32,16,4096]{2,1,0:T(8,128)(2,1)S(1)} fusion(f32[32,16]{1,0:T(8,128)S(1)} %bitcast.105, bf16[32,16,4096]{2,1,0:T(8,128)(2,1)} %copy-done.1), kind=kLoop, calls=%fused_computation.2 | loop fusion | flops 6291456 | bytes 8390656 | tf_op jit(solution)/shard_map/convert_element_type | solution.py:49
  102.8 2.0 copy-done.2
  104.8 5.6 %convolution_convert_fusion = bf16[768,4096]{1,0:T(8,128)(2,1)} fusion(bf16[512,4096]{1,0:T(8,128)(2,1)S(1)} %bitcast.103, bf16[1,1,512,768]{3,2,1,0:T(8,128)(2,1)S(1)} %copy-done.7, bf16[1,1,512,768]{3,2,1,0:T(8,128)(2,1)S(1)} %copy-done.6), kind=kOutput, calls=%fused_computation.3 | convolution fusion | flops 3227516928 | bytes 12058624 | tf_op jit(solution)/shard_map/dot_general | solution.py:59
  110.5 0.7 copy-done.5
  111.2 0.1 copy.53
  111.3 0.1 copy.54
  111.4 0.4 select_reduce_fusion
  111.8 1.7 fusion.4
  113.4 1.8 copy.55
  115.3 1.8 copy.56
  117.1 45.7 %all_to_all.39 = f32[8,32,16,128]{3,2,0,1:T(8,128)S(1)} all-to-all(f32[8,32,16,128]{3,2,0,1:T(8,128)S(1)} %copy.56), channel_id=1, replica_groups=mesh['dp'=8,'expert'=32] {'expert'}, dimensions={1} | all-to-all | bytes 4194304 | tf_op jit(solution)/shard_map/all_to_all | solution.py:80
  162.7 0.8 reduce_sum.78
  163.5 17.8 %all-to-all-start.4 = ((f32[8,16,128]{2,1,0:T(8,128)}), f32[8,16,128]{2,1,0:T(8,128)S(1)}, u32[]{:S(2)}, u32[]{:S(2)}) async-start(f32[8,16,128]{2,1,0:T(8,128)} %reduce_sum.78), calls=%async_computation.5 | async-start | bytes 131072 | tf_op jit(solution)/shard_map/all_to_all | solution.py:82
  181.3 9.5 %fusion.25 = (bf16[1,1,512,768]{3,2,1,0:T(8,128)(2,1)}, bf16[1,1,512,768]{3,2,1,0:T(8,128)(2,1)}) fusion(bf16[1,1,512,768]{3,2,1,0:T(8,128)(2,1)} %param.10, bf16[1,1,512,768]{3,2,1,0:T(8,128)(2,1)} %param.11, bf16[512,4096]{1,0:T(8,128)(2,1)} %bitcast.104, bf16[1,768,4096]{2,1,0:T(8,128)(2,1)} %param.12), kind=kOutput, calls=%fused_computation.36 | convolution fusion | flops 3227123712 | bytes 13631488 | tf_op jit(solution)/shard_map/dot_general | solution.py:52
  190.8 0.6 reduce_sum.79
  191.4 16.8 %reduce-scatter.2.cloned.1.call-done = bf16[96,4096]{1,0:T(8,128)(2,1)} async-done(((bf16[768,4096]{1,0:T(8,128)(2,1)}), bf16[96,4096]{1,0:T(8,128)(2,1)}) %reduce-scatter.2.cloned.1.call-update) | async-done | bytes 786448 | tf_op jit(solution)/shard_map/reduce_scatter | solution.py:58
  208.2 2.4 %bitcast_convert_fusion = f32[1,96,4096]{2,1,0:T(8,128)} fusion(bf16[96,4096]{1,0:T(8,128)(2,1)} %reduce-scatter.2.cloned.1.call-done), kind=kLoop, calls=%fused_computation.33 | loop fusion | flops 393216 | bytes 2359296 | tf_op jit(solution)/shard_map/broadcast_in_dim | solution.py:84
  (30 shorter events, 0.3 us)
Async XLA Ops:
  7.2 1.9 copy-start
  7.2 201.0 %reduce-scatter.2.cloned.1.call-start = ((), (), s32[]{:S(2)}) async-start(), calls=%async_computation.6 | async-start | bytes 7077888 | tf_op jit(solution)/shard_map/reduce_scatter | solution.py:58
  9.1 61.1 %slice-start = ((s8[6291456]{0:T(1024)(128)(4,1)}), s8[4194304]{0:T(1024)(128)(4,1)S(1)}, s32[]{:S(2)}) async-start(s8[6291456]{0:T(1024)(128)(4,1)} %bitcast.109), calls=%async_computation.7 | async-start | bytes 8388608
  10.4 59.8 %slice-start.1 = ((s8[6291456]{0:T(1024)(128)(4,1)}), s8[2097152]{0:T(1024)(128)(4,1)S(1)}, s32[]{:S(2)}) async-start(s8[6291456]{0:T(1024)(128)(4,1)} %bitcast.109), calls=%async_computation.8 | async-start | bytes 4194304
  10.4 59.8 %copy-start.6 = (bf16[1,1,512,768]{3,2,1,0:T(8,128)(2,1)S(1)}, bf16[1,1,512,768]{3,2,1,0:T(8,128)(2,1)}, u32[]{:S(2)}) copy-start(bf16[1,1,512,768]{3,2,1,0:T(8,128)(2,1)} %param.10) | copy-start | bytes 2359300
  10.4 59.8 %copy-start.7 = (bf16[1,1,512,768]{3,2,1,0:T(8,128)(2,1)S(1)}, bf16[1,1,512,768]{3,2,1,0:T(8,128)(2,1)}, u32[]{:S(2)}) copy-start(bf16[1,1,512,768]{3,2,1,0:T(8,128)(2,1)} %param.11) | copy-start | bytes 2359300
  68.2 1.9 copy-start.1
  70.2 18.2 %copy-start.3 = (f32[128,8]{0,1:T(8,128)S(1)}, f32[128,8]{0,1:T(8,128)}, u32[]{:S(2)}) copy-start(f32[128,8]{0,1:T(8,128)} %param.9) | copy-start | bytes 12292
  88.4 22.9 %copy-start.4 = (f32[128,8]{0,1:T(8,128)}, f32[128,8]{0,1:T(8,128)S(1)}, u32[]{:S(2)}) copy-start(f32[128,8]{0,1:T(8,128)S(1)} %get-tuple-element.5) | copy-start | bytes 12292
  102.8 2.0 copy-start.2
  110.5 0.7 copy-start.5
  163.5 27.3 %all-to-all-start.4 = ((f32[8,16,128]{2,1,0:T(8,128)}), f32[8,16,128]{2,1,0:T(8,128)S(1)}, u32[]{:S(2)}, u32[]{:S(2)}) async-start(f32[8,16,128]{2,1,0:T(8,128)} %reduce_sum.78), calls=%async_computation.5 | async-start | bytes 131072 | tf_op jit(solution)/shard_map/all_to_all | solution.py:82
Sparse Core Ops, SparseCore 0:
  110.6 97.5 reduce-scatter.1

commit v2 on v0

v2 whole, which is shorter than its diff:
```python
import functools

import jax
import jax.numpy as jnp
from jax import lax
from jax.experimental import pallas as pl
from jax.experimental.pallas import tpu as pltpu
from jax.sharding import PartitionSpec as P

EXP_DEV = 4
TOK = 128
TOPK = 8
D = 4096
FFE = 768
SLOTS = 512
HALF = SLOTS // 2
EXPERTS = 128
MOST = 16
NC = 4
DC = D // NC
DH = DC // 2
OWN = FFE // 8
MESH = pl.DeviceIdType.MESH
F32 = jnp.float32
BF = jnp.bfloat16


def dot(a, b, ca=1, cb=0):
    return lax.dot_general(a, b, (((ca,), (cb,)), ((), ())), preferred_element_type=F32)


def m16(index):
    return pl.multiple_of(index * 16, 16)


def body(
    tok, ids, rw, gate_hbm, up_hbm, w_hbm, moe_hbm,
    gate_out, up_out, down_out, route_out, router_out,
    gate, up, w, moe, moe_t, placer, placer_t, placer_p, tok_p, weight_by_expert,
    w_send, w_recv, snd, recv, hidden, active, gate_factor, hw_t, hc,
    term, pair, psum, ring, back_send, back_recv,
    prod, prod_b, rp, rq_send, rq, rz_send, rz, gate_v, up_v, down_v,
    in_sem, z_s, z_r, w_s, w_r, a_s, a_r, p_s, p_r, g_s, g_r, b_s, b_r,
    rp_s, rp_r, rq_s, rq_r, rz_s, rz_r, out_sem,
):
    d = lax.axis_index("dp")
    e = lax.axis_index("expert")
    zhi, core = d // 2, d % 2
    zlo, yx = e // 16, e % 16
    y, x = yx // 4, yx % 4
    sibling = (zhi * 2 + 1 - core, e)
    partner = (d, (1 - zlo) * 16 + yx)
    up_ring = (((zhi + 1) % 4) * 2 + core, e)
    down_ring = (((zhi + 3) % 4) * 2 + core, e)
    z = zhi * 2 + zlo

    def column(k):
        other = (z + k) % 8
        return other, ((other // 2) * 2 + core, (other % 2) * 16 + yx)

    def plane(k):
        step = (k * 5) % 16
        return ((y + step // 4) % 4) * 4 + (x + step % 4) % 4

    def send(src, dst, s, r, target):
        pltpu.make_async_remote_copy(src, dst, s, r, target, MESH).start()

    def drain(ref, sem):
        pltpu.make_async_copy(ref, ref, sem).wait()

    bar = pltpu.get_barrier_semaphore()

    def greet(k, carry):
        pl.semaphore_signal(bar, inc=1, device_id=(d, (e + k) % 32), device_id_type=MESH)
        return carry

    lax.fori_loop(1, 32, greet, 0)
    pl.semaphore_signal(bar, inc=1, device_id=sibling, device_id_type=MESH)

    def greet_column(k, carry):
        pl.semaphore_signal(
            bar, inc=1, device_id=(((zhi + k) % 4) * 2 + core, e), device_id_type=MESH
        )
        pl.semaphore_signal(
            bar, inc=1, device_id=(((zhi + k) % 4) * 2 + core, (1 - zlo) * 16 + yx), device_id_type=MESH
        )
        return carry

    lax.fori_loop(1, 4, greet_column, 0)

    loads = [
        pltpu.make_async_copy(gate_hbm, gate, in_sem.at[0]),
        pltpu.make_async_copy(up_hbm, up, in_sem.at[1]),
        pltpu.make_async_copy(moe_hbm, moe, in_sem.at[2]),
        pltpu.make_async_copy(w_hbm, w, in_sem.at[3]),
    ]
    for load in loads:
        load.start()

    lane = lax.broadcasted_iota(jnp.int32, (TOK, EXPERTS), 1)
    row = lax.broadcasted_iota(jnp.int32, (TOK, EXPERTS), 0)
    named = jnp.zeros((TOK, EXPERTS), F32)
    weights = jnp.zeros((TOK, EXPERTS), F32)
    for k in range(TOPK):
        match = ids[:, k : k + 1] == lane
        named = named + jnp.where(match, 1.0, 0.0)
        weights = weights + jnp.where(match, rw[:, k : k + 1], 0.0)
    weight_by_expert[...] = weights
    before = jnp.where(lane < row, 1.0, 0.0).astype(BF)
    rank = dot(before, named.astype(BF))
    code = (named * (rank + 1.0)).astype(BF)
    slot_row = lax.broadcasted_iota(jnp.int32, (SLOTS, EXPERTS), 0)
    slot_lane = lax.broadcasted_iota(jnp.int32, (SLOTS, EXPERTS), 1)
    chooser = jnp.where(slot_lane == EXP_DEV * (slot_row // MOST), 1.0, 0.0)
    chooser_b = chooser.astype(BF)
    placed = dot(chooser_b, code, 1, 1) == (slot_row % MOST + 1).astype(F32)
    placer[...] = jnp.where(placed, 1.0, 0.0).astype(BF)
    slot_weights = jnp.sum(jnp.where(placed, dot(chooser_b, weights.astype(BF), 1, 1), 0.0), 1, keepdims=True)
    w_send[...] = jnp.broadcast_to(slot_weights, (SLOTS, 128)).astype(BF)
    t_row = lax.broadcasted_iota(jnp.int32, (EXPERTS, SLOTS), 0)
    t_col = lax.broadcasted_iota(jnp.int32, (EXPERTS, SLOTS), 1)
    chooser_t = jnp.where(t_row == EXP_DEV * (t_col // MOST), 1.0, 0.0).astype(BF)
    placed_t = dot(code, chooser_t) == (
        lax.broadcasted_iota(jnp.int32, (TOK, SLOTS), 1) % MOST + 1
    ).astype(F32)
    placer_t[...] = jnp.where(placed_t, 1.0, 0.0).astype(BF)

    pl.semaphore_wait(bar, 38)

    send(placer.at[pl.ds(pl.multiple_of((1 - zlo) * HALF, HALF), HALF)], placer_p, z_s, z_r.at[NC], partner)
    for c in range(NC):
        cols = pl.ds(c * DC, DC)
        send(tok.at[:, cols], tok_p.at[:, cols], z_s, z_r.at[c], partner)

    def pack(half, c):
        cols = pl.ds(c * DC, DC)
        if half == 0:
            chosen = placer[pl.ds(pl.multiple_of(zlo * HALF, HALF), HALF), :]
            tokens = tok
        else:
            chosen = placer_p[...]
            tokens = tok_p
        for q in range(DC // 256):
            part = pl.ds(c * DC + q * 256, 256)
            snd[pl.ds(half * HALF, HALF), part] = dot(chosen, tokens[:, part]).astype(BF)
        source = zlo * 16 + yx if half == 0 else (1 - zlo) * 16 + yx
        recv[pl.ds(m16(source), 16), cols] = snd[pl.ds(m16(half * 16 + yx), 16), cols]

        def one(k, carry):
            target = plane(k)
            send(
                snd.at[pl.ds(m16(half * 16 + target), 16), cols],
                recv.at[pl.ds(m16(source), 16), cols],
                a_s, a_r.at[c, half], (d, zlo * 16 + target),
            )
            return carry

        lax.fori_loop(1, 16, one, 0)

    def pack_partner(c):
        drain(tok_p.at[:, pl.ds(c * DC, DC)], z_r.at[c])
        pack(1, c)

    pack(0, 0)

    w_recv[pl.ds(m16(e), 16), :] = w_send[pl.ds(m16(e), 16), :]

    def give_weight(k, carry):
        target = (e + k) % 32
        send(w_send.at[pl.ds(m16(target), 16)], w_recv.at[pl.ds(m16(e), 16)], w_s, w_r, (d, target))
        return carry

    lax.fori_loop(1, 32, give_weight, 0)

    pack(0, 1)

    loads[0].wait()
    loads[1].wait()

    def gates(i, carry):
        part = pl.ds(pl.multiple_of(i * 32, 32), 32)
        g = gate[part, :].astype(F32)
        u = up[part, :].astype(F32)
        sigma = jax.nn.sigmoid(g)
        act = g * sigma
        active[part, :] = act
        gate_factor[part, :] = u * sigma * (1.0 + g * (1.0 - sigma))
        hidden[part, :] = (act * u).astype(BF)
        return carry

    lax.fori_loop(0, SLOTS // 32, gates, 0)

    drain(placer_p, z_r.at[NC])
    pack_partner(0)
    pack(0, 2)

    loads[2].wait()

    def turn(i, carry):
        part = pl.ds(pl.multiple_of(i * 512, 512), 512)
        moe_t[part, :] = moe[:, part].T
        return carry

    lax.fori_loop(0, D // 512, turn, 0)

    drain(w_recv.at[pl.ds(0, SLOTS - 16)], w_r)

    def weigh(i, carry):
        part = pl.ds(pl.multiple_of(i * 128, 128), 128)
        scale = jnp.concatenate([w_recv[part, :].astype(F32)] * (FFE // 128), axis=1)
        hw_t[:, part] = (scale * hidden[part, :].astype(F32)).astype(BF).T
        return carry

    lax.fori_loop(0, SLOTS // 128, weigh, 0)

    pack_partner(1)
    pack(0, 3)
    loads[3].wait()

    def arrive(c):
        for half in range(2):
            drain(recv.at[pl.ds(0, HALF - 16), pl.ds(c * DC, DC)], a_r.at[c, half])

    def make_term(c):
        def one(q, carry):
            inner = pl.ds(pl.multiple_of(q * 256, 256), 256)
            outer = pl.ds(pl.multiple_of(c * DC + q * 256, 256), 256)
            block = dot(hw_t[...], recv[:, outer]).astype(BF)
            term[c, :, :, inner] = block.reshape(8, OWN, 256)
            return carry

        lax.fori_loop(0, DC // 256, one, 0)

        def give(k, carry):
            send(term.at[c, 2 * k + 1 - core], pair.at[c, k], p_s, p_r.at[c], sibling)
            return carry

        lax.fori_loop(0, 4, give, 0)

    def make_hidden(c):
        cols = pl.ds(c * DC, DC)

        def one(q, carry):
            part = pl.ds(pl.multiple_of(q * 256, 256), 256)
            block = dot(recv[:, cols], w[part, cols], 1, 1)
            if c == 0:
                hc[:, part] = block
            else:
                hc[:, part] = hc[:, part] + block
            return carry

        lax.fori_loop(0, FFE // 256, one, 0)

    left, right = pl.ds(0, DH), pl.ds(DH, DH)

    def ring_send(c, step, first, second):
        send(first, ring.at[c, step, 0], g_s, g_r.at[c, step, 0], up_ring)
        send(second, ring.at[c, step, 1], g_s, g_r.at[c, step, 1], down_ring)

    def pair_sum(c):
        drain(pair.at[c], p_r.at[c])

        def one(k, carry):
            psum[c, k] = (term[c, 2 * k + core].astype(F32) + pair[c, k].astype(F32)).astype(BF)
            return carry

        lax.fori_loop(0, 4, one, 0)
        ring_send(
            c, 0, psum.at[c, (zhi + 3) % 4, :, left], psum.at[c, (zhi + 1) % 4, :, right]
        )

    def ring_step(c, step):
        for way, half, index in ((0, left, (zhi + 6 - step) % 4), (1, right, (zhi + 2 + step) % 4)):
            drain(ring.at[c, step, way], g_r.at[c, step, way])
            total = ring[c, step, way].astype(F32) + psum[c, index, :, half].astype(F32)
            ring[c, step, way] = total.astype(BF)
        ring_send(c, step + 1, ring.at[c, step, 0], ring.at[c, step, 1])

    outs = [
        pltpu.make_async_copy(gate_v, gate_out, out_sem.at[0]),
        pltpu.make_async_copy(up_v, up_out, out_sem.at[1]),
    ]
    down_outs = [
        pltpu.make_async_copy(
            down_v.at[:, pl.ds(c * DC, DC)], down_out.at[:, pl.ds(c * DC, DC)], out_sem.at[2 + c]
        )
        for c in range(NC)
    ]

    def ring_end(c):
        for way, half in ((0, left), (1, right)):
            drain(ring.at[c, 2, way], g_r.at[c, 2, way])
            total = ring[c, 2, way].astype(F32) + psum[c, zhi, :, half].astype(F32)
            down_v[:, pl.ds(c * DC + way * DH, DH)] = total
        down_outs[c].start()

    def progress(c, stage):
        if stage == 0:
            pair_sum(c)
        elif stage < 3:
            ring_step(c, stage - 1)
        else:
            ring_end(c)

    arrive(0)
    make_term(0)
    pack_partner(2)
    make_hidden(0)
    progress(0, 0)
    pack_partner(3)

    arrive(1)
    make_term(1)
    progress(0, 1)
    make_hidden(1)
    progress(1, 0)
    progress(0, 2)

    arrive(2)
    make_term(2)
    progress(1, 1)
    make_hidden(2)
    progress(2, 0)
    progress(0, 3)
    progress(1, 2)

    arrive(3)
    make_term(3)
    progress(2, 1)
    make_hidden(3)

    def dots(i, carry):
        part = pl.ds(pl.multiple_of(i * 32, 32), 32)
        value = jnp.sum(hidden[part, :].astype(F32) * hc[part, :], 1, keepdims=True)
        back_send[part, :] = jnp.broadcast_to(value, (32, 128))
        return carry

    lax.fori_loop(0, SLOTS // 32, dots, 0)
    back_recv[pl.ds(m16(e), 16), :] = back_send[pl.ds(m16(e), 16), :]

    def give_back(k, carry):
        target = (e + k) % 32
        send(back_send.at[pl.ds(m16(target), 16)], back_recv.at[pl.ds(m16(e), 16)], b_s, b_r, (d, target))
        return carry

    lax.fori_loop(1, 32, give_back, 0)
    progress(3, 0)

    def grads(i, carry):
        part = pl.ds(pl.multiple_of(i * 32, 32), 32)
        scale = jnp.concatenate([w_recv[part, :].astype(F32)] * (FFE // 128), axis=1)
        cot = hc[part, :] * scale
        up_v[part, :] = (cot * active[part, :]).astype(BF)
        gate_v[part, :] = (cot * gate_factor[part, :]).astype(BF)
        return carry

    lax.fori_loop(0, SLOTS // 32, grads, 0)
    outs[0].start()
    outs[1].start()
    progress(1, 3)

    drain(back_recv.at[pl.ds(0, SLOTS - 16)], b_r)
    spread = back_recv[...] * chooser
    high = spread.astype(BF)
    rest = spread - high.astype(F32)
    middle = rest.astype(BF)
    low = (rest - middle.astype(F32)).astype(BF)
    by_expert = dot(placer_t[...], high) + dot(placer_t[...], middle) + dot(placer_t[...], low)
    column8 = lax.broadcasted_iota(jnp.int32, (TOK, TOPK), 1)
    routes = jnp.zeros((TOK, TOPK), F32)
    for k in range(TOPK):
        found = jnp.sum(jnp.where(ids[:, k : k + 1] == lane, by_expert, 0.0), 1, keepdims=True)
        routes = jnp.where(column8 == k, found, routes)
    route_out[...] = routes
    mine = weight_by_expert[...]
    mixed = jnp.sum(mine * by_expert, 1, keepdims=True)
    logit = (mine * (by_expert - mixed)).astype(BF)

    def product(i, carry):
        block = dot(moe_t[pl.ds(pl.multiple_of(i * 512, 512), 512), :], logit)
        prod[i] = block
        prod_b[i] = block.astype(BF)
        return carry

    lax.fori_loop(0, 8, product, 0)

    def give_pair(k, carry):
        send(prod_b.at[2 * k + 1 - core], rp.at[k], rp_s, rp_r, sibling)
        return carry

    lax.fori_loop(0, 4, give_pair, 0)
    progress(2, 2)
    progress(3, 1)

    drain(rp, rp_r)

    def pair_router(k, carry):
        both = prod[2 * k + core] + rp[k].astype(F32)
        rq_send[pl.ds(2 * k, 2)] = both.astype(BF).reshape(2, HALF, 128)
        return carry

    lax.fori_loop(0, 4, pair_router, 0)
    rq[yx] = rq_send[:, pl.ds(m16(yx), 16), :]

    def give_plane(k, carry):
        target = plane(k)
        send(rq_send.at[:, pl.ds(m16(target), 16)], rq.at[yx], rq_s, rq_r, (d, zlo * 16 + target))
        return carry

    lax.fori_loop(1, 16, give_plane, 0)
    progress(2, 3)
    drain(rq.at[pl.ds(0, 15)], rq_r)

    def add_plane(k, total):
        return total + rq[k].astype(F32)

    rz_send[...] = lax.fori_loop(1, 16, add_plane, rq[0].astype(F32)).astype(BF)
    rz[z] = rz_send[z]

    def give_column(k, carry):
        other, target = column(k)
        send(rz_send.at[other], rz.at[z], rz_s, rz_r, target)
        return carry

    lax.fori_loop(1, 8, give_column, 0)
    progress(3, 2)
    drain(rz.at[pl.ds(0, 7)], rz_r)
    total = rz[0].astype(F32)
    for k in range(1, 8):
        total = total + rz[k].astype(F32)
    router_out[...] = 0.015625 * total
    progress(3, 3)

    drain(placer_p, z_s)
    drain(tok_p, z_s)
    drain(w_recv.at[pl.ds(0, SLOTS - 16)], w_s)
    drain(recv.at[pl.ds(0, SLOTS - 32)], a_s)
    drain(pair, p_s)
    drain(ring, g_s)
    drain(back_recv.at[pl.ds(0, SLOTS - 16)], b_s)
    drain(rp, rp_s)
    drain(rq.at[pl.ds(0, 15)], rq_s)
    drain(rz.at[pl.ds(0, 7)], rz_s)
    outs[0].wait()
    outs[1].wait()
    for copy in down_outs:
        copy.wait()


def per_device(out_cot, route_ids, route_weight, saved_gate, saved_up, down_weight, moe_input):
    vmem = pl.BlockSpec(memory_space=pltpu.VMEM)
    anywhere = pl.BlockSpec(memory_space=pl.ANY)
    dma = pltpu.SemaphoreType.DMA
    scratch = [
        ((SLOTS, FFE), BF),
        ((SLOTS, FFE), BF),
        ((FFE, D), BF),
        ((TOK, D), BF),
        ((D, TOK), BF),
        ((SLOTS, TOK), BF),
        ((TOK, SLOTS), BF),
        ((HALF, TOK), BF),
        ((TOK, D), BF),
        ((TOK, EXPERTS), F32),
        ((SLOTS, 128), BF),
        ((SLOTS, 128), BF),
        ((SLOTS, D), BF),
        ((SLOTS, D), BF),
        ((SLOTS, FFE), BF),
        ((SLOTS, FFE), F32),
        ((SLOTS, FFE), F32),
        ((FFE, SLOTS), BF),
        ((SLOTS, FFE), F32),
        ((NC, 8, OWN, DC), BF),
        ((NC, 4, OWN, DC), BF),
        ((NC, 4, OWN, DC), BF),
        ((NC, 3, 2, OWN, DH), BF),
        ((SLOTS, 128), F32),
        ((SLOTS, 128), F32),
        ((8, 512, 128), F32),
        ((8, 512, 128), BF),
        ((4, 512, 128), BF),
        ((8, HALF, 128), BF),
        ((16, 8, 16, 128), BF),
        ((8, 16, 128), BF),
        ((8, 16, 128), BF),
        ((SLOTS, FFE), BF),
        ((SLOTS, FFE), BF),
        ((OWN, D), F32),
    ]
    sems = [
        dma((4,)), dma(()), dma((NC + 1,)), dma(()), dma(()), dma(()), dma((NC, 2)),
        dma(()), dma((NC,)), dma(()), dma((NC, 3, 2)), dma(()), dma(()),
        dma(()), dma(()), dma(()), dma(()), dma(()), dma(()), dma((2 + NC,)),
    ]
    outs = pl.pallas_call(
        body,
        out_shape=(
            jax.ShapeDtypeStruct((SLOTS, FFE), BF),
            jax.ShapeDtypeStruct((SLOTS, FFE), BF),
            jax.ShapeDtypeStruct((OWN, D), F32),
            jax.ShapeDtypeStruct((TOK, TOPK), F32),
            jax.ShapeDtypeStruct((16, EXPERTS), F32),
        ),
        in_specs=[vmem] * 3 + [anywhere] * 4,
        out_specs=(anywhere, anywhere, anywhere, vmem, vmem),
        scratch_shapes=[pltpu.VMEM(shape, kind) for shape, kind in scratch] + sems,
        compiler_params=pltpu.CompilerParams(
            collective_id=0, has_side_effects=True, vmem_limit_bytes=58 * 2**20
        ),
    )(out_cot, route_ids, route_weight, saved_gate[0, 0], saved_up[0, 0], down_weight[0], moe_input)
    gate_grad, up_grad, down_grad, route_grad, router_grad = outs
    return gate_grad[None, None], up_grad[None, None], down_grad[None], route_grad, router_grad


def solution(mesh):
    placed = (
        P(("dp", "expert"), None),
        P(("dp", "expert"), None),
        P(("dp", "expert"), None),
        P("dp", "expert", None, None),
        P("dp", "expert", None, None),
        P("expert", None, None),
        P(("dp", "expert"), None),
    )
    return jax.shard_map(
        per_device,
        mesh=mesh,
        in_specs=placed,
        out_specs=(
            P("dp", "expert", None, None),
            P("dp", "expert", None, None),
            P("expert", "dp", None),
            P(("dp", "expert"), None),
            P(("dp", "expert"), None),
        ),
        check_vma=False,
    )
```

time: 1470 us -> 127 us (0.09)
  the two profiles are of different devices: /device:TPU:0 before, /device:TPU:1 now
where the time goes in v2:
time: 127 us
  Pallas kernels  117 us (92%)
  local copies, waits for them, and re-layouts  9.22 us (7%)
    pallas_call x1, Pallas kernels, per_device(): pl.pallas_call(body, out_shape=(jax.ShapeDtypeStruct((SLOTS, FFE), BF), j...  117 us
    unnamed x13, local copies, waits for them, and re-layouts  9.22 us

profile of v2, /device:TPU:1, one launch (start us, length us, event | category | flops | bytes accessed | tf_op | source)
XLA Modules:
  0.0 126.9 jit_solution(10049026867881567896)
XLA Ops:
  0.6 1.4 %copy.12.ids = s32[128,8]{1,0:T(8,128)} copy(s32[128,8]{0,1:T(8,128)} %param.8) | data formatting | bytes 8192 | tf_op args[1]
  2.0 1.4 %copy.13.rw = f32[128,8]{1,0:T(8,128)} copy(f32[128,8]{0,1:T(8,128)} %param.9) | data formatting | bytes 8192 | tf_op args[2]
  3.5 117.0 %shard_map.110 = (bf16[512,768]{1,0:T(8,128)(2,1)}, bf16[512,768]{1,0:T(8,128)(2,1)}, f32[96,4096]{1,0:T(8,128)}, f32[128,8]{1,0:T(8,128)}, f32[16,128]{1,0:T(8,128)}) custom-call(bf16[128,4096]{1,0:T(8,128)(2,1)} %tok.1, s32[128,8]{1,0:T(8,128)} %copy.12.ids, f32[128,8]{1,0:T(8,128)} %copy.13.rw, bf16[512,768]{1,0:T(8,128)(2,1)} %bitcast.8, ...), custom_call_target="tpu_custom_call" | custom-call | tf_op jit(solution)/shard_map/pallas_call | solution.py:496
  120.5 0.0 copy-start.1
  120.5 1.6 %copy.14 = f32[128,8]{0,1:T(8,128)} copy(f32[128,8]{1,0:T(8,128)} %get-tuple-element.18) | data formatting | bytes 8192
  122.0 0.0 copy-start
  122.0 2.2 %copy.19 = bf16[1,1,512,768]{3,2,1,0:T(8,128)(2,1)} copy(bf16[1,1,512,768]{3,2,1,0:T(8,128)(2,1)} %bitcast.11) | data formatting | bytes 1572864
  124.2 0.0 copy-done.1
  124.2 0.9 copy.20
  125.1 0.0 copy-done
  125.1 0.0 copy-start.2
  125.1 1.1 copy.21
  126.3 0.0 copy-done.2
  126.3 0.6 copy.22
Async XLA Ops:
  120.5 3.8 %copy-start.1 = (bf16[512,768]{1,0:T(8,128)(2,1)S(1)}, bf16[512,768]{1,0:T(8,128)(2,1)}, u32[]{:S(2)}) copy-start(bf16[512,768]{1,0:T(8,128)(2,1)} %get-tuple-element.11) | copy-start | bytes 2359300
  122.0 3.1 %copy-start = (f32[96,4096]{1,0:T(8,128)S(1)}, f32[96,4096]{1,0:T(8,128)}, u32[]{:S(2)}) copy-start(f32[96,4096]{1,0:T(8,128)} %get-tuple-element.12) | copy-start | bytes 4718596
  125.1 1.1 copy-start.2

commit v3 on v2

v3 whole, which is shorter than its diff:
```python
import functools

import jax
import jax.numpy as jnp
from jax import lax
from jax.experimental import pallas as pl
from jax.experimental.pallas import tpu as pltpu
from jax.sharding import PartitionSpec as P

EXP_DEV = 4
TOK = 128
TOPK = 8
D = 4096
FFE = 768
SLOTS = 512
HALF = SLOTS // 2
EXPERTS = 128
MOST = 16
NC = 8
DC = D // NC
DH = DC // 2
OWN = FFE // 8
MESH = pl.DeviceIdType.MESH
F32 = jnp.float32
BF = jnp.bfloat16


def dot(a, b, ca=1, cb=0):
    return lax.dot_general(a, b, (((ca,), (cb,)), ((), ())), preferred_element_type=F32)


def m16(index):
    return pl.multiple_of(index * 16, 16)


def body(
    tok_hbm, ids_hbm, rw_hbm, gate_hbm, up_hbm, w_hbm, moe_hbm,
    gate_out, up_out, down_out, route_out, router_out,
    tok, ids, rw, gate, up, w, moe, moe_t, placer, placer_p, tok_p, weight_by_expert,
    w_send, w_recv, snd, recv, hidden, active, gate_factor, hw_t, hc,
    term, pair, psum, ring, back_send, back_recv,
    prod, prod_b, rp, rq_send, rq, rz_send, rz, gate_v, up_v, down_v, route_v, router_v,
    in_sem, z_s, z_r, w_s, w_r, a_s, a_r, p_s, p_r, g_s, g_r, b_s, b_r,
    rp_s, rp_r, rq_s, rq_r, rz_s, rz_r, out_sem, logit,
):
    d = lax.axis_index("dp")
    e = lax.axis_index("expert")
    zhi, core = d // 2, d % 2
    zlo, yx = e // 16, e % 16
    y, x = yx // 4, yx % 4
    sibling = (zhi * 2 + 1 - core, e)
    partner = (d, (1 - zlo) * 16 + yx)
    up_ring = (((zhi + 1) % 4) * 2 + core, e)
    down_ring = (((zhi + 3) % 4) * 2 + core, e)
    z = zhi * 2 + zlo

    def column(k):
        other = (z + k) % 8
        return other, ((other // 2) * 2 + core, (other % 2) * 16 + yx)

    def plane(k):
        step = (k * 5) % 16
        return ((y + step // 4) % 4) * 4 + (x + step % 4) % 4

    def send(src, dst, s, r, target):
        pltpu.make_async_remote_copy(src, dst, s, r, target, MESH).start()

    def drain(ref, sem):
        pltpu.make_async_copy(ref, ref, sem).wait()

    bar = pltpu.get_barrier_semaphore()

    def greet(k, carry):
        pl.semaphore_signal(bar, inc=1, device_id=(d, (e + k) % 32), device_id_type=MESH)
        return carry

    lax.fori_loop(1, 32, greet, 0)
    pl.semaphore_signal(bar, inc=1, device_id=sibling, device_id_type=MESH)

    def greet_column(k, carry):
        pl.semaphore_signal(
            bar, inc=1, device_id=(((zhi + k) % 4) * 2 + core, e), device_id_type=MESH
        )
        pl.semaphore_signal(
            bar, inc=1, device_id=(((zhi + k) % 4) * 2 + core, (1 - zlo) * 16 + yx), device_id_type=MESH
        )
        return carry

    lax.fori_loop(1, 4, greet_column, 0)

    loads = [
        pltpu.make_async_copy(source, here, in_sem.at[i])
        for i, (source, here) in enumerate(
            (
                (ids_hbm, ids), (rw_hbm, rw), (tok_hbm, tok), (gate_hbm, gate),
                (up_hbm, up), (moe_hbm, moe), (w_hbm, w),
            )
        )
    ]
    for load in loads:
        load.start()
    load_ids, load_rw, load_tok, load_gate, load_up, load_moe, load_w = loads
    load_ids.wait()
    load_rw.wait()

    expert_row = lax.broadcasted_iota(jnp.int32, (EXPERTS, TOK), 0)
    token_lane = lax.broadcasted_iota(jnp.int32, (EXPERTS, TOK), 1)
    named = jnp.zeros((EXPERTS, TOK), F32)
    weights = jnp.zeros((EXPERTS, TOK), F32)
    for k in range(TOPK):
        match = ids[k : k + 1, :] == expert_row
        named = named + jnp.where(match, 1.0, 0.0)
        weights = weights + jnp.where(match, rw[k : k + 1, :], 0.0)
    weight_by_expert[...] = weights
    before = jnp.where(expert_row < token_lane, 1.0, 0.0).astype(BF)
    rank = dot(named.astype(BF), before)
    code = (named * (rank + 1.0)).astype(BF)
    slot_row = lax.broadcasted_iota(jnp.int32, (SLOTS, EXPERTS), 0)
    slot_lane = lax.broadcasted_iota(jnp.int32, (SLOTS, EXPERTS), 1)
    chooser = jnp.where(slot_lane == EXP_DEV * (slot_row // MOST), 1.0, 0.0)
    chooser_b = chooser.astype(BF)
    placed = dot(chooser_b, code) == (slot_row % MOST + 1).astype(F32)
    placer[...] = jnp.where(placed, 1.0, 0.0).astype(BF)
    slot_weights = jnp.sum(
        jnp.where(placed, dot(chooser_b, weights.astype(BF)), 0.0), 1, keepdims=True
    )
    w_send[...] = jnp.broadcast_to(slot_weights, (SLOTS, 128)).astype(BF)
    load_tok.wait()

    pl.semaphore_wait(bar, 38)

    w_recv[pl.ds(m16(e), 16), :] = w_send[pl.ds(m16(e), 16), :]

    def give_weight(k, carry):
        target = (e + k) % 32
        send(w_send.at[pl.ds(m16(target), 16)], w_recv.at[pl.ds(m16(e), 16)], w_s, w_r, (d, target))
        return carry

    lax.fori_loop(1, 32, give_weight, 0)

    send(placer.at[pl.ds(pl.multiple_of((1 - zlo) * HALF, HALF), HALF)], placer_p, z_s, z_r.at[NC], partner)
    for c in range(NC):
        cols = pl.ds(c * DC, DC)
        send(tok.at[:, cols], tok_p.at[:, cols], z_s, z_r.at[c], partner)

    def pack(half, c):
        cols = pl.ds(c * DC, DC)
        if half == 0:
            chosen = placer[pl.ds(pl.multiple_of(zlo * HALF, HALF), HALF), :]
            tokens = tok
        else:
            chosen = placer_p[...]
            tokens = tok_p
        for q in range(DC // 256):
            part = pl.ds(c * DC + q * 256, 256)
            snd[pl.ds(half * HALF, HALF), part] = dot(chosen, tokens[:, part]).astype(BF)
        source = zlo * 16 + yx if half == 0 else (1 - zlo) * 16 + yx
        recv[pl.ds(m16(source), 16), cols] = snd[pl.ds(m16(half * 16 + yx), 16), cols]

        def one(k, carry):
            target = plane(k)
            send(
                snd.at[pl.ds(m16(half * 16 + target), 16), cols],
                recv.at[pl.ds(m16(source), 16), cols],
                a_s, a_r.at[c, half], (d, zlo * 16 + target),
            )
            return carry

        lax.fori_loop(1, 16, one, 0)

    def pack_partner(c):
        if c == 0:
            drain(placer_p, z_r.at[NC])
        drain(tok_p.at[:, pl.ds(c * DC, DC)], z_r.at[c])
        pack(1, c)

    def gates(i, carry):
        part = pl.ds(pl.multiple_of(i * 32, 32), 32)
        g = gate[part, :].astype(F32)
        u = up[part, :].astype(F32)
        sigma = jax.nn.sigmoid(g)
        act = g * sigma
        active[part, :] = act
        gate_factor[part, :] = u * sigma * (1.0 + g * (1.0 - sigma))
        hidden[part, :] = (act * u).astype(BF)
        return carry

    def make_gates():
        load_gate.wait()
        load_up.wait()
        lax.fori_loop(0, SLOTS // 32, gates, 0)

    def turn(i, carry):
        part = pl.ds(pl.multiple_of(i * 512, 512), 512)
        moe_t[part, :] = moe[:, part].T
        return carry

    def turn_moe():
        load_moe.wait()
        lax.fori_loop(0, D // 512, turn, 0)

    def weigh(i, carry):
        part = pl.ds(pl.multiple_of(i * 128, 128), 128)
        scale = jnp.concatenate([w_recv[part, :].astype(F32)] * (FFE // 128), axis=1)
        hw_t[:, part] = (scale * hidden[part, :].astype(F32)).astype(BF).T
        return carry

    def weigh_hidden():
        drain(w_recv.at[pl.ds(0, SLOTS - 16)], w_r)
        lax.fori_loop(0, SLOTS // 128, weigh, 0)

    def arrive(c):
        for half in range(2):
            drain(recv.at[pl.ds(0, HALF - 16), pl.ds(c * DC, DC)], a_r.at[c, half])

    def make_term(c):
        arrive(c)
        for q in range(DC // 256):
            cols = pl.ds(c * DC + q * 256, 256)
            block = dot(hw_t[...], recv[:, cols]).astype(BF)
            term[:, :, :, cols] = block.reshape(4, 2, OWN, 256)
        cols = pl.ds(c * DC, DC)
        send(term.at[:, 1 - core, :, cols], pair.at[:, :, cols], p_s, p_r.at[c], sibling)

    def make_hidden(c):
        if c == 1:
            load_w.wait()
        cols = pl.ds((c - 1) * DC, 2 * DC)

        def one(q, carry):
            part = pl.ds(pl.multiple_of(q * 256, 256), 256)
            block = dot(recv[:, cols], w[part, cols], 1, 1)
            if c == 1:
                hc[:, part] = block
            else:
                hc[:, part] = hc[:, part] + block
            return carry

        lax.fori_loop(0, FFE // 256, one, 0)

    def ways(c):
        return (
            (0, pl.ds(c * DC, DH), up_ring, 1),
            (1, pl.ds(c * DC + DH, DH), down_ring, -1),
        )

    def pair_sum(c):
        cols = pl.ds(c * DC, DC)
        drain(pair.at[:, :, cols], p_r.at[c])

        def one(k, carry):
            both = term[k, core, :, cols].astype(F32) + pair[k, :, cols].astype(F32)
            psum[k, :, cols] = both.astype(BF)
            return carry

        lax.fori_loop(0, 4, one, 0)
        for way, part, target, sign in ways(c):
            block = (zhi + 4 - sign) % 4
            send(psum.at[block, :, part], ring.at[0, :, part], g_s, g_r.at[c, 0, way], target)

    def ring_step(c, step):
        for way, part, target, sign in ways(c):
            drain(ring.at[step, :, part], g_r.at[c, step, way])
            block = (zhi + 8 - sign * (step + 2)) % 4
            total = ring[step, :, part].astype(F32) + psum[block, :, part].astype(F32)
            ring[step, :, part] = total.astype(BF)
            send(ring.at[step, :, part], ring.at[step + 1, :, part], g_s, g_r.at[c, step + 1, way], target)

    outs = [
        pltpu.make_async_copy(gate_v, gate_out, out_sem.at[0]),
        pltpu.make_async_copy(up_v, up_out, out_sem.at[1]),
        pltpu.make_async_copy(route_v, route_out, out_sem.at[2]),
        pltpu.make_async_copy(router_v, router_out, out_sem.at[3]),
    ]
    down_outs = [
        pltpu.make_async_copy(
            down_v.at[:, pl.ds(c * DC, DC)], down_out.at[:, pl.ds(c * DC, DC)], out_sem.at[4 + c]
        )
        for c in range(NC)
    ]

    def ring_end(c):
        for way, part, target, sign in ways(c):
            drain(ring.at[2, :, part], g_r.at[c, 2, way])
            down_v[:, part] = ring[2, :, part].astype(F32) + psum[zhi, :, part].astype(F32)
        down_outs[c].start()

    def dots(i, carry):
        part = pl.ds(pl.multiple_of(i * 32, 32), 32)
        value = jnp.sum(hidden[part, :].astype(F32) * hc[part, :], 1, keepdims=True)
        back_send[part, :] = jnp.broadcast_to(value, (32, 128))
        return carry

    def give_back(k, carry):
        target = (e + k) % 32
        send(back_send.at[pl.ds(m16(target), 16)], back_recv.at[pl.ds(m16(e), 16)], b_s, b_r, (d, target))
        return carry

    def give_dots():
        lax.fori_loop(0, SLOTS // 32, dots, 0)
        back_recv[pl.ds(m16(e), 16), :] = back_send[pl.ds(m16(e), 16), :]
        lax.fori_loop(1, 32, give_back, 0)

    def grads(i, carry):
        part = pl.ds(pl.multiple_of(i * 32, 32), 32)
        scale = jnp.concatenate([w_recv[part, :].astype(F32)] * (FFE // 128), axis=1)
        cot = hc[part, :] * scale
        up_v[part, :] = (cot * active[part, :]).astype(BF)
        gate_v[part, :] = (cot * gate_factor[part, :]).astype(BF)
        return carry

    def make_grads():
        lax.fori_loop(0, SLOTS // 32, grads, 0)
        outs[0].start()
        outs[1].start()

    def product(i, carry):
        block = dot(moe_t[pl.ds(pl.multiple_of(i * 512, 512), 512), :], logit[...], 1, 1)
        prod[i] = block
        prod_b[i] = block.astype(BF)
        return carry

    def give_pair(k, carry):
        send(prod_b.at[2 * k + 1 - core], rp.at[k], rp_s, rp_r, sibling)
        return carry

    def router_terms():
        drain(back_recv.at[pl.ds(0, SLOTS - 16)], b_r)
        spread = (back_recv[...] * chooser).T
        high = spread.astype(BF)
        rest = spread - high.astype(F32)
        middle = rest.astype(BF)
        low = (rest - middle.astype(F32)).astype(BF)
        by_expert = dot(high, placer[...]) + dot(middle, placer[...]) + dot(low, placer[...])
        for k in range(TOPK):
            picked = jnp.where(ids[k : k + 1, :] == expert_row, by_expert, 0.0)
            route_v[k : k + 1, :] = jnp.sum(picked, 0, keepdims=True)
        outs[2].start()
        mine = weight_by_expert[...]
        mixed = jnp.sum(mine * by_expert, 0, keepdims=True)
        logit[...] = (mine * (by_expert - mixed)).astype(BF)
        lax.fori_loop(0, 8, product, 0)
        lax.fori_loop(0, 4, give_pair, 0)

    def pair_router(k, carry):
        both = prod[2 * k + core] + rp[k].astype(F32)
        rq_send[pl.ds(2 * k, 2)] = both.astype(BF).reshape(2, HALF, 128)
        return carry

    def give_plane(k, carry):
        target = plane(k)
        send(rq_send.at[:, pl.ds(m16(target), 16)], rq.at[yx], rq_s, rq_r, (d, zlo * 16 + target))
        return carry

    def router_pair():
        drain(rp, rp_r)
        lax.fori_loop(0, 4, pair_router, 0)
        rq[yx] = rq_send[:, pl.ds(m16(yx), 16), :]
        lax.fori_loop(1, 16, give_plane, 0)

    def add_plane(k, total):
        return total + rq[k].astype(F32)

    def give_column(k, carry):
        other, target = column(k)
        send(rz_send.at[other], rz.at[z], rz_s, rz_r, target)
        return carry

    def router_plane():
        drain(rq.at[pl.ds(0, 15)], rq_r)
        rz_send[...] = lax.fori_loop(1, 16, add_plane, rq[0].astype(F32)).astype(BF)
        rz[z] = rz_send[z]
        lax.fori_loop(1, 8, give_column, 0)

    def router_end():
        drain(rz.at[pl.ds(0, 7)], rz_r)
        total = rz[0].astype(F32)
        for k in range(1, 8):
            total = total + rz[k].astype(F32)
        router_v[...] = 0.015625 * total
        outs[3].start()

    pack(0, 0)
    pack(0, 1)
    make_gates()
    turn_moe()
    pack_partner(0)
    pack(0, 2)
    weigh_hidden()
    pack_partner(1)
    pack(0, 3)
    pack_partner(2)
    pack(0, 4)
    make_term(0)
    pack_partner(3)
    pack(0, 5)
    pair_sum(0)
    pack_partner(4)
    pack(0, 6)
    make_term(1)
    make_hidden(1)
    pack_partner(5)
    pack(0, 7)
    pair_sum(1)
    pack_partner(6)
    make_term(2)
    pack_partner(7)
    pair_sum(2)
    ring_step(0, 0)
    make_term(3)
    ring_step(1, 0)
    make_hidden(3)
    ring_step(2, 0)
    pair_sum(3)
    ring_step(0, 1)
    make_term(4)
    ring_step(1, 1)
    pair_sum(4)
    ring_step(2, 1)
    ring_step(3, 0)
    make_term(5)
    make_hidden(5)
    ring_end(0)
    pair_sum(5)
    ring_end(1)
    make_term(6)
    ring_step(4, 0)
    ring_end(2)
    make_term(7)
    pair_sum(6)
    make_hidden(7)
    ring_step(3, 1)
    give_dots()
    ring_step(5, 0)
    pair_sum(7)
    make_grads()
    ring_step(4, 1)
    ring_step(6, 0)
    ring_end(3)
    router_terms()
    ring_step(5, 1)
    ring_step(7, 0)
    router_pair()
    ring_end(4)
    ring_step(6, 1)
    ring_end(5)
    ring_step(7, 1)
    router_plane()
    ring_end(6)
    ring_end(7)
    router_end()
    drain(placer_p, z_s)
    drain(tok_p, z_s)
    drain(w_recv.at[pl.ds(0, SLOTS - 16)], w_s)
    drain(recv.at[pl.ds(0, SLOTS - 32)], a_s)
    drain(pair, p_s)
    drain(ring, g_s)
    drain(back_recv.at[pl.ds(0, SLOTS - 16)], b_s)
    drain(rp, rp_s)
    drain(rq.at[pl.ds(0, 15)], rq_s)
    drain(rz.at[pl.ds(0, 7)], rz_s)
    for copy in outs + down_outs:
        copy.wait()


def per_device(out_cot, route_ids, route_weight, saved_gate, saved_up, down_weight, moe_input):
    anywhere = pl.BlockSpec(memory_space=pl.ANY)
    dma = pltpu.SemaphoreType.DMA
    scratch = [
        ((TOK, D), BF),
        ((TOPK, TOK), jnp.int32),
        ((TOPK, TOK), F32),
        ((SLOTS, FFE), BF),
        ((SLOTS, FFE), BF),
        ((FFE, D), BF),
        ((TOK, D), BF),
        ((D, TOK), BF),
        ((SLOTS, TOK), BF),
        ((HALF, TOK), BF),
        ((TOK, D), BF),
        ((EXPERTS, TOK), F32),
        ((SLOTS, 128), BF),
        ((SLOTS, 128), BF),
        ((SLOTS, D), BF),
        ((SLOTS, D), BF),
        ((SLOTS, FFE), BF),
        ((SLOTS, FFE), F32),
        ((SLOTS, FFE), F32),
        ((FFE, SLOTS), BF),
        ((SLOTS, FFE), F32),
        ((4, 2, OWN, D), BF),
        ((4, OWN, D), BF),
        ((4, OWN, D), BF),
        ((3, OWN, D), BF),
        ((SLOTS, 128), F32),
        ((SLOTS, 128), F32),
        ((8, 512, 128), F32),
        ((8, 512, 128), BF),
        ((4, 512, 128), BF),
        ((8, HALF, 128), BF),
        ((16, 8, 16, 128), BF),
        ((8, 16, 128), BF),
        ((8, 16, 128), BF),
        ((SLOTS, FFE), BF),
        ((SLOTS, FFE), BF),
        ((OWN, D), F32),
        ((TOPK, TOK), F32),
        ((16, EXPERTS), F32),
    ]
    sems = [
        dma((7,)), dma(()), dma((NC + 1,)), dma(()), dma(()), dma(()), dma((NC, 2)),
        dma(()), dma((NC,)), dma(()), dma((NC, 3, 2)), dma(()), dma(()),
        dma(()), dma(()), dma(()), dma(()), dma(()), dma(()), dma((4 + NC,)),
        pltpu.VMEM((EXPERTS, TOK), BF),
    ]
    outs = pl.pallas_call(
        body,
        out_shape=(
            jax.ShapeDtypeStruct((SLOTS, FFE), BF),
            jax.ShapeDtypeStruct((SLOTS, FFE), BF),
            jax.ShapeDtypeStruct((OWN, D), F32),
            jax.ShapeDtypeStruct((TOPK, TOK), F32),
            jax.ShapeDtypeStruct((16, EXPERTS), F32),
        ),
        in_specs=[anywhere] * 7,
        out_specs=(anywhere,) * 5,
        scratch_shapes=[pltpu.VMEM(shape, kind) for shape, kind in scratch] + sems,
        compiler_params=pltpu.CompilerParams(
            collective_id=0, has_side_effects=True, vmem_limit_bytes=58 * 2**20
        ),
    )(
        out_cot, route_ids.T, route_weight.T, saved_gate[0, 0], saved_up[0, 0],
        down_weight[0], moe_input,
    )
    gate_grad, up_grad, down_grad, route_grad, router_grad = hand_over(outs)
    return gate_grad[None, None], up_grad[None, None], down_grad[None], route_grad.T, router_grad


def hand_over_body(*refs):
    sources, targets, held, load_sem, store_sem = refs[:5], refs[5:10], refs[10:15], refs[15], refs[16]
    loads, stores = [], []
    for source, target, here in zip(sources, targets, held):
        pieces = 4 if source.shape[0] >= 64 else 1
        rows = source.shape[0] // pieces
        for i in range(pieces):
            part, n = pl.ds(i * rows, rows), len(loads)
            loads.append(pltpu.make_async_copy(source.at[part], here.at[part], load_sem.at[n]))
            stores.append(pltpu.make_async_copy(here.at[part], target.at[part], store_sem.at[n]))
    for load in loads:
        load.start()
    for load, store in zip(loads, stores):
        load.wait()
        store.start()
    for store in stores:
        store.wait()


def hand_over(arrays):
    anywhere = pl.BlockSpec(memory_space=pl.ANY)
    return pl.pallas_call(
        hand_over_body,
        out_shape=[jax.ShapeDtypeStruct(a.shape, a.dtype) for a in arrays],
        in_specs=[anywhere] * 5,
        out_specs=[anywhere] * 5,
        scratch_shapes=[pltpu.VMEM(a.shape, a.dtype) for a in arrays]
        + [pltpu.SemaphoreType.DMA((14,))] * 2,
        compiler_params=pltpu.CompilerParams(vmem_limit_bytes=58 * 2**20),
    )(*arrays)


def solution(mesh):
    placed = (
        P(("dp", "expert"), None),
        P(("dp", "expert"), None),
        P(("dp", "expert"), None),
        P("dp", "expert", None, None),
        P("dp", "expert", None, None),
        P("expert", None, None),
        P(("dp", "expert"), None),
    )
    return jax.shard_map(
        per_device,
        mesh=mesh,
        in_specs=placed,
        out_specs=(
            P("dp", "expert", None, None),
            P("dp", "expert", None, None),
            P("expert", "dp", None),
            P(("dp", "expert"), None),
            P(("dp", "expert"), None),
        ),
        check_vma=False,
    )
```

time: 127 us -> 105 us (0.83)
  Pallas kernels: 117 us -> 104 us
  local copies, waits for them, and re-layouts: 9.22 us -> 0 us
    pallas_call x1, Pallas kernels: 117 us -> 101 us  [per_device(): pl.pallas_call(body, out_shape=(jax.ShapeDtypeStruct((SLOTS, FFE), BF), j...]
    unnamed x13 -> x0, local copies, waits for them, and re-layouts: 9.22 us -> none
    pallas_call x0 -> x1, Pallas kernels: none -> 3.22 us  [hand_over(): pl.pallas_call(hand_over_body, out_shape=[jax.ShapeDtypeStruct(a.shape, a...]
where the time goes in v3:
time: 105 us
  Pallas kernels  104 us (99%)
    pallas_call x1, Pallas kernels, per_device(): pl.pallas_call(body, out_shape=(jax.ShapeDtypeStruct((SLOTS, FFE), BF), j...  101 us
    pallas_call x1, Pallas kernels, hand_over(): pl.pallas_call(hand_over_body, out_shape=[jax.ShapeDtypeStruct(a.shape, a...  3.22 us

profile of v3, /device:TPU:1, one launch (start us, length us, event | category | flops | bytes accessed | tf_op | source)
XLA Modules:
  0.0 104.6 jit_solution(3766780779988030861)
XLA Ops:
  0.6 100.7 %shard_map.110 = (bf16[512,768]{1,0:T(8,128)(2,1)}, bf16[512,768]{1,0:T(8,128)(2,1)}, f32[96,4096]{1,0:T(8,128)}, f32[8,128]{1,0:T(8,128)}, f32[16,128]{1,0:T(8,128)}) custom-call(bf16[128,4096]{1,0:T(8,128)(2,1)} %tok_hbm.1, s32[8,128]{1,0:T(8,128)} %bitcast.12, f32[8,128]{1,0:T(8,128)} %bitcast.13, bf16[512,768]{1,0:T(8,128)(2,1)} %bitcast.10, ...), custom_call_target="tpu_custom_call" | custom-call | tf_op jit(solution)/shard_map/pallas_call | solution.py:516
  101.4 3.2 %shard_map.111 = (bf16[512,768]{1,0:T(8,128)(2,1)}, bf16[512,768]{1,0:T(8,128)(2,1)}, f32[96,4096]{1,0:T(8,128)}, f32[8,128]{1,0:T(8,128)}, f32[16,128]{1,0:T(8,128)}) custom-call(bf16[512,768]{1,0:T(8,128)(2,1)} %get-tuple-element.15.refs_0_, bf16[512,768]{1,0:T(8,128)(2,1)} %get-tuple-element.16.refs_1_, f32[96,4096]{1,0:T(8,128)} %get-tuple-element.17.refs_2_, ...), custom_call_target="tpu_custom_call" | custom-call | tf_op jit(solution)/shard_map/pallas_call | solution.py:560

commit v4 on v3

--- a/solution.py
+++ b/solution.py
@@ -36,7 +36,7 @@
 def body(
     tok_hbm, ids_hbm, rw_hbm, gate_hbm, up_hbm, w_hbm, moe_hbm,
     gate_out, up_out, down_out, route_out, router_out,
-    tok, ids, rw, gate, up, w, moe, moe_t, placer, placer_p, tok_p, weight_by_expert,
+    tok, ids, rw, gate, up, w, moe, moe_t, placer, meta, meta_p, flying_code, tok_p, weight_by_expert,
     w_send, w_recv, snd, recv, hidden, active, gate_factor, hw_t, hc,
     term, pair, psum, ring, back_send, back_recv,
     prod, prod_b, rp, rq_send, rq, rz_send, rz, gate_v, up_v, down_v, route_v, router_v,
@@ -115,42 +115,43 @@
     before = jnp.where(expert_row < token_lane, 1.0, 0.0).astype(BF)
     rank = dot(named.astype(BF), before)
     code = (named * (rank + 1.0)).astype(BF)
-    slot_row = lax.broadcasted_iota(jnp.int32, (SLOTS, EXPERTS), 0)
-    slot_lane = lax.broadcasted_iota(jnp.int32, (SLOTS, EXPERTS), 1)
-    chooser = jnp.where(slot_lane == EXP_DEV * (slot_row // MOST), 1.0, 0.0)
-    chooser_b = chooser.astype(BF)
-    placed = dot(chooser_b, code) == (slot_row % MOST + 1).astype(F32)
-    placer[...] = jnp.where(placed, 1.0, 0.0).astype(BF)
-    slot_weights = jnp.sum(
-        jnp.where(placed, dot(chooser_b, weights.astype(BF)), 0.0), 1, keepdims=True
-    )
-    w_send[...] = jnp.broadcast_to(slot_weights, (SLOTS, 128)).astype(BF)
+    flying_row = lax.broadcasted_iota(jnp.int32, (32, EXPERTS), 0)
+    flying_lane = lax.broadcasted_iota(jnp.int32, (32, EXPERTS), 1)
+    flying = jnp.where(flying_lane == EXP_DEV * flying_row, 1.0, 0.0).astype(BF)
+    codes = dot(flying, code)
+    flying_code[...] = codes
+    flying_weight = dot(flying, weights.astype(BF)).astype(BF)
+    meta[0, :16] = codes[:16].astype(BF)
+    meta[0, 16:] = flying_weight[:16]
+    meta[1, :16] = codes[16:].astype(BF)
+    meta[1, 16:] = flying_weight[16:]
+
+    half_row = lax.broadcasted_iota(jnp.int32, (HALF, 32), 0)
+    half_lane = lax.broadcasted_iota(jnp.int32, (HALF, 32), 1)
+    to_code = jnp.where(half_lane == half_row // MOST, 1.0, 0.0).astype(BF)
+    to_weight = jnp.where(half_lane == 16 + half_row // MOST, 1.0, 0.0).astype(BF)
+    place = (lax.broadcasted_iota(jnp.int32, (HALF, TOK), 0) % MOST + 1).astype(F32)
+
+    def lay_out(half, about):
+        placed = dot(to_code, about) == place
+        placer[half] = jnp.where(placed, 1.0, 0.0).astype(BF)
+        total = jnp.sum(jnp.where(placed, dot(to_weight, about), 0.0), 1, keepdims=True)
+        w_send[half] = jnp.broadcast_to(total, (HALF, 128)).astype(BF)
+
+    lay_out(0, meta[zlo])
     load_tok.wait()
 
     pl.semaphore_wait(bar, 38)
 
-    w_recv[pl.ds(m16(e), 16), :] = w_send[pl.ds(m16(e), 16), :]
-
-    def give_weight(k, carry):
-        target = (e + k) % 32
-        send(w_send.at[pl.ds(m16(target), 16)], w_recv.at[pl.ds(m16(e), 16)], w_s, w_r, (d, target))
-        return carry
-
-    lax.fori_loop(1, 32, give_weight, 0)
-
-    send(placer.at[pl.ds(pl.multiple_of((1 - zlo) * HALF, HALF), HALF)], placer_p, z_s, z_r.at[NC], partner)
+    send(meta.at[1 - zlo], meta_p, z_s, z_r.at[NC], partner)
     for c in range(NC):
         cols = pl.ds(c * DC, DC)
         send(tok.at[:, cols], tok_p.at[:, cols], z_s, z_r.at[c], partner)
 
     def pack(half, c):
         cols = pl.ds(c * DC, DC)
-        if half == 0:
-            chosen = placer[pl.ds(pl.multiple_of(zlo * HALF, HALF), HALF), :]
-            tokens = tok
-        else:
-            chosen = placer_p[...]
-            tokens = tok_p
+        chosen = placer[half]
+        tokens = tok if half == 0 else tok_p
         for q in range(DC // 256):
             part = pl.ds(c * DC + q * 256, 256)
             snd[pl.ds(half * HALF, HALF), part] = dot(chosen, tokens[:, part]).astype(BF)
@@ -168,9 +169,26 @@
 
         lax.fori_loop(1, 16, one, 0)
 
+    def give_weights(half):
+        source = zlo * 16 + yx if half == 0 else (1 - zlo) * 16 + yx
+        w_recv[pl.ds(m16(source), 16), :] = w_send[half, pl.ds(m16(yx), 16), :]
+
+        def one(k, carry):
+            target = plane(k)
+            send(
+                w_send.at[half, pl.ds(m16(target), 16)], w_recv.at[pl.ds(m16(source), 16)],
+                w_s, w_r, (d, zlo * 16 + target),
+            )
+            return carry
+
+        lax.fori_loop(1, 16, one, 0)
+
+    def read_partner():
+        drain(meta_p, z_r.at[NC])
+        lay_out(1, meta_p[...])
+        give_weights(1)
+
     def pack_partner(c):
-        if c == 0:
-            drain(placer_p, z_r.at[NC])
         drain(tok_p.at[:, pl.ds(c * DC, DC)], z_r.at[c])
         pack(1, c)
 
@@ -206,7 +224,7 @@
         return carry
 
     def weigh_hidden():
-        drain(w_recv.at[pl.ds(0, SLOTS - 16)], w_r)
+        drain(w_recv.at[pl.ds(0, SLOTS - 32)], w_r)
         lax.fori_loop(0, SLOTS // 128, weigh, 0)
 
     def arrive(c):
@@ -286,19 +304,22 @@
         down_outs[c].start()
 
     def dots(i, carry):
-        part = pl.ds(pl.multiple_of(i * 32, 32), 32)
-        value = jnp.sum(hidden[part, :].astype(F32) * hc[part, :], 1, keepdims=True)
-        back_send[part, :] = jnp.broadcast_to(value, (32, 128))
+        part = pl.ds(pl.multiple_of(i * 128, 128), 128)
+        total = jnp.zeros((128, 128), F32)
+        for q in range(FFE // 128):
+            cols = pl.ds(q * 128, 128)
+            total = total + hidden[part, cols].astype(F32) * hc[part, cols]
+        back_send[i] = jnp.sum(total.T, 0, keepdims=True)
         return carry
 
     def give_back(k, carry):
         target = (e + k) % 32
-        send(back_send.at[pl.ds(m16(target), 16)], back_recv.at[pl.ds(m16(e), 16)], b_s, b_r, (d, target))
+        send(back_send.at[target // 8], back_recv.at[e], b_s, b_r, (d, target))
         return carry
 
     def give_dots():
-        lax.fori_loop(0, SLOTS // 32, dots, 0)
-        back_recv[pl.ds(m16(e), 16), :] = back_send[pl.ds(m16(e), 16), :]
+        lax.fori_loop(0, SLOTS // 128, dots, 0)
+        back_recv[e] = back_send[e // 8]
         lax.fori_loop(1, 32, give_back, 0)
 
     def grads(i, carry):
@@ -325,13 +346,20 @@
         return carry
 
     def router_terms():
-        drain(back_recv.at[pl.ds(0, SLOTS - 16)], b_r)
-        spread = (back_recv[...] * chooser).T
-        high = spread.astype(BF)
-        rest = spread - high.astype(F32)
+        drain(back_recv.at[pl.ds(0, 31)], b_r)
+        back = jnp.concatenate([back_recv[j] for j in range(32)], axis=0)
+        back = pltpu.roll(back, (8 - e % 8) % 8 * 16, 1)
+        flown = jnp.zeros((32, TOK), F32)
+        for r in range(MOST):
+            flown = flown + jnp.where(flying_code[...] == r + 1.0, back[:, r : r + 1], 0.0)
+        stretch_row = lax.broadcasted_iota(jnp.int32, (EXPERTS, 32), 0)
+        stretch_lane = lax.broadcasted_iota(jnp.int32, (EXPERTS, 32), 1)
+        stretch = jnp.where(stretch_row == EXP_DEV * stretch_lane, 1.0, 0.0).astype(BF)
+        high = flown.astype(BF)
+        rest = flown - high.astype(F32)
         middle = rest.astype(BF)
         low = (rest - middle.astype(F32)).astype(BF)
-        by_expert = dot(high, placer[...]) + dot(middle, placer[...]) + dot(low, placer[...])
+        by_expert = dot(stretch, high) + dot(stretch, middle) + dot(stretch, low)
         for k in range(TOPK):
             picked = jnp.where(ids[k : k + 1, :] == expert_row, by_expert, 0.0)
             route_v[k : k + 1, :] = jnp.sum(picked, 0, keepdims=True)
@@ -382,7 +410,9 @@
 
     pack(0, 0)
     pack(0, 1)
+    give_weights(0)
     make_gates()
+    read_partner()
     turn_moe()
     pack_partner(0)
     pack(0, 2)
@@ -401,61 +431,62 @@
     make_hidden(1)
     pack_partner(5)
     pack(0, 7)
+    pack_partner(6)
     pair_sum(1)
-    pack_partner(6)
     make_term(2)
     pack_partner(7)
+    ring_step(0, 0)
     pair_sum(2)
-    ring_step(0, 0)
+    ring_step(1, 0)
     make_term(3)
-    ring_step(1, 0)
     make_hidden(3)
+    ring_step(0, 1)
     ring_step(2, 0)
     pair_sum(3)
-    ring_step(0, 1)
+    ring_step(1, 1)
     make_term(4)
-    ring_step(1, 1)
+    ring_end(0)
+    ring_step(2, 1)
     pair_sum(4)
-    ring_step(2, 1)
     ring_step(3, 0)
     make_term(5)
     make_hidden(5)
-    ring_end(0)
+    ring_end(1)
+    ring_end(2)
     pair_sum(5)
-    ring_end(1)
+    ring_step(4, 0)
     make_term(6)
-    ring_step(4, 0)
-    ring_end(2)
+    ring_step(3, 1)
     make_term(7)
+    make_hidden(7)
+    give_dots()
     pair_sum(6)
-    make_hidden(7)
-    ring_step(3, 1)
-    give_dots()
+    ring_step(4, 1)
+    pair_sum(7)
     ring_step(5, 0)
-    pair_sum(7)
+    ring_end(3)
     make_grads()
-    ring_step(4, 1)
+    router_terms()
     ring_step(6, 0)
-    ring_end(3)
-    router_terms()
-    ring_step(5, 1)
+    ring_end(4)
     ring_step(7, 0)
     router_pair()
-    ring_end(4)
+    ring_step(5, 1)
     ring_step(6, 1)
+    ring_step(7, 1)
     ring_end(5)
-    ring_step(7, 1)
     router_plane()
     ring_end(6)
     ring_end(7)
     router_end()
-    drain(placer_p, z_s)
+
+    drain(meta_p, z_s)
     drain(tok_p, z_s)
-    drain(w_recv.at[pl.ds(0, SLOTS - 16)], w_s)
+    drain(w_recv.at[pl.ds(0, SLOTS - 32)], w_s)
     drain(recv.at[pl.ds(0, SLOTS - 32)], a_s)
     drain(pair, p_s)
     drain(ring, g_s)
-    drain(back_recv.at[pl.ds(0, SLOTS - 16)], b_s)
+    drain(back_recv.at[pl.ds(0, 31)], b_s)
     drain(rp, rp_s)
     drain(rq.at[pl.ds(0, 15)], rq_s)
     drain(rz.at[pl.ds(0, 7)], rz_s)
@@ -475,11 +506,13 @@
         ((FFE, D), BF),
         ((TOK, D), BF),
         ((D, TOK), BF),
-        ((SLOTS, TOK), BF),
-        ((HALF, TOK), BF),
+        ((2, HALF, TOK), BF),
+        ((2, 32, TOK), BF),
+        ((32, TOK), BF),
+        ((32, TOK), F32),
         ((TOK, D), BF),
         ((EXPERTS, TOK), F32),
-        ((SLOTS, 128), BF),
+        ((2, HALF, 128), BF),
         ((SLOTS, 128), BF),
         ((SLOTS, D), BF),
         ((SLOTS, D), BF),
@@ -492,8 +525,8 @@
         ((4, OWN, D), BF),
         ((4, OWN, D), BF),
         ((3, OWN, D), BF),
-        ((SLOTS, 128), F32),
-        ((SLOTS, 128), F32),
+        ((4, 1, 128), F32),
+        ((32, 1, 128), F32),
         ((8, 512, 128), F32),
         ((8, 512, 128), BF),
         ((4, 512, 128), BF),

time: 105 us -> 96.3 us (0.917)
  Pallas kernels: 104 us -> 95.5 us
    pallas_call x1, Pallas kernels: 101 us -> 92.3 us  [per_device(): pl.pallas_call(body, out_shape=(jax.ShapeDtypeStruct((SLOTS, FFE), BF), j...]
where the time goes in v4:
time: 96.3 us; the launch traced here: 96.2 us
  Pallas kernels  95.5 us (99%)
    pallas_call x1, Pallas kernels, per_device(): pl.pallas_call(body, out_shape=(jax.ShapeDtypeStruct((SLOTS, FFE), BF), j...  92.3 us
    pallas_call x1, Pallas kernels, hand_over(): pl.pallas_call(hand_over_body, out_shape=[jax.ShapeDtypeStruct(a.shape, a...  3.22 us

profile of v4, /device:TPU:1, one launch (start us, length us, event | category | flops | bytes accessed | tf_op | source)
XLA Modules:
  0.0 96.2 jit_solution(15222596488918982927)
XLA Ops:
  0.6 92.3 %shard_map.110 = (bf16[512,768]{1,0:T(8,128)(2,1)}, bf16[512,768]{1,0:T(8,128)(2,1)}, f32[96,4096]{1,0:T(8,128)}, f32[8,128]{1,0:T(8,128)}, f32[16,128]{1,0:T(8,128)}) custom-call(bf16[128,4096]{1,0:T(8,128)(2,1)} %tok_hbm.1, s32[8,128]{1,0:T(8,128)} %bitcast.12, f32[8,128]{1,0:T(8,128)} %bitcast.13, bf16[512,768]{1,0:T(8,128)(2,1)} %bitcast.10, ...), custom_call_target="tpu_custom_call" | custom-call | tf_op jit(solution)/shard_map/pallas_call | solution.py:549
  93.0 3.2 %shard_map.111 = (bf16[512,768]{1,0:T(8,128)(2,1)}, bf16[512,768]{1,0:T(8,128)(2,1)}, f32[96,4096]{1,0:T(8,128)}, f32[8,128]{1,0:T(8,128)}, f32[16,128]{1,0:T(8,128)}) custom-call(bf16[512,768]{1,0:T(8,128)(2,1)} %get-tuple-element.15.refs_0_, bf16[512,768]{1,0:T(8,128)(2,1)} %get-tuple-element.16.refs_1_, f32[96,4096]{1,0:T(8,128)} %get-tuple-element.17.refs_2_, ...), custom_call_target="tpu_custom_call" | custom-call | tf_op jit(solution)/shard_map/pallas_call | solution.py:593

commit v5 on v4

--- a/solution.py
+++ b/solution.py
@@ -243,7 +243,8 @@
     def make_hidden(c):
         if c == 1:
             load_w.wait()
-        cols = pl.ds((c - 1) * DC, 2 * DC)
+        first = c - 1 if c < NC - 2 else c
+        cols = pl.ds(first * DC, (c + 1 - first) * DC)
 
         def one(q, carry):
             part = pl.ds(pl.multiple_of(q * 256, 256), 256)
@@ -335,14 +336,16 @@
         outs[0].start()
         outs[1].start()
 
-    def product(i, carry):
-        block = dot(moe_t[pl.ds(pl.multiple_of(i * 512, 512), 512), :], logit[...], 1, 1)
-        prod[i] = block
-        prod_b[i] = block.astype(BF)
-        return carry
-
-    def give_pair(k, carry):
-        send(prod_b.at[2 * k + 1 - core], rp.at[k], rp_s, rp_r, sibling)
+    def product(i):
+        return dot(moe_t[pl.ds(pl.multiple_of(i * 512, 512), 512), :], logit[...], 1, 1)
+
+    def product_sibling(k, carry):
+        prod_b[k] = product(2 * k + 1 - core).astype(BF)
+        send(prod_b.at[k], rp.at[k], rp_s, rp_r, sibling)
+        return carry
+
+    def product_own(k, carry):
+        prod[k] = product(2 * k + core)
         return carry
 
     def router_terms():
@@ -367,11 +370,11 @@
         mine = weight_by_expert[...]
         mixed = jnp.sum(mine * by_expert, 0, keepdims=True)
         logit[...] = (mine * (by_expert - mixed)).astype(BF)
-        lax.fori_loop(0, 8, product, 0)
-        lax.fori_loop(0, 4, give_pair, 0)
+        lax.fori_loop(0, 4, product_sibling, 0)
+        lax.fori_loop(0, 4, product_own, 0)
 
     def pair_router(k, carry):
-        both = prod[2 * k + core] + rp[k].astype(F32)
+        both = prod[k] + rp[k].astype(F32)
         rq_send[pl.ds(2 * k, 2)] = both.astype(BF).reshape(2, HALF, 128)
         return carry
 
@@ -432,53 +435,54 @@
     pack_partner(5)
     pack(0, 7)
     pack_partner(6)
+    make_term(2)
     pair_sum(1)
-    make_term(2)
     pack_partner(7)
+    pair_sum(2)
     ring_step(0, 0)
-    pair_sum(2)
-    ring_step(1, 0)
     make_term(3)
     make_hidden(3)
-    ring_step(0, 1)
+    ring_step(1, 0)
     ring_step(2, 0)
     pair_sum(3)
+    ring_step(0, 1)
+    make_term(4)
     ring_step(1, 1)
-    make_term(4)
-    ring_end(0)
     ring_step(2, 1)
     pair_sum(4)
-    ring_step(3, 0)
     make_term(5)
     make_hidden(5)
+    ring_step(3, 0)
+    pair_sum(5)
+    ring_end(0)
+    make_term(6)
+    make_hidden(6)
     ring_end(1)
-    ring_end(2)
-    pair_sum(5)
-    ring_step(4, 0)
-    make_term(6)
-    ring_step(3, 1)
     make_term(7)
     make_hidden(7)
     give_dots()
     pair_sum(6)
-    ring_step(4, 1)
+    ring_step(3, 1)
+    ring_step(4, 0)
     pair_sum(7)
     ring_step(5, 0)
-    ring_end(3)
+    ring_end(2)
     make_grads()
     router_terms()
     ring_step(6, 0)
-    ring_end(4)
+    ring_step(4, 1)
+    router_pair()
+    ring_end(3)
     ring_step(7, 0)
-    router_pair()
     ring_step(5, 1)
     ring_step(6, 1)
+    router_plane()
     ring_step(7, 1)
+    ring_end(4)
+    router_end()
     ring_end(5)
-    router_plane()
     ring_end(6)
     ring_end(7)
-    router_end()
 
     drain(meta_p, z_s)
     drain(tok_p, z_s)
@@ -527,8 +531,8 @@
         ((3, OWN, D), BF),
         ((4, 1, 128), F32),
         ((32, 1, 128), F32),
-        ((8, 512, 128), F32),
-        ((8, 512, 128), BF),
+        ((4, 512, 128), F32),
+        ((4, 512, 128), BF),
         ((4, 512, 128), BF),
         ((8, HALF, 128), BF),
         ((16, 8, 16, 128), BF),

time: 96.3 us -> 95.3 us (0.990)
  Pallas kernels: 95.5 us -> 94.5 us
    pallas_call x1, Pallas kernels: 92.3 us -> 91.3 us  [per_device(): pl.pallas_call(body, out_shape=(jax.ShapeDtypeStruct((SLOTS, FFE), BF), j...]
where the time goes in v5:
time: 95.3 us; the launch traced here: 95.1 us
  Pallas kernels  94.5 us (99%)
    pallas_call x1, Pallas kernels, per_device(): pl.pallas_call(body, out_shape=(jax.ShapeDtypeStruct((SLOTS, FFE), BF), j...  91.3 us
    pallas_call x1, Pallas kernels, hand_over(): pl.pallas_call(hand_over_body, out_shape=[jax.ShapeDtypeStruct(a.shape, a...  3.22 us

profile of v5, /device:TPU:1, one launch (start us, length us, event | category | flops | bytes accessed | tf_op | source)
XLA Modules:
  0.0 95.1 jit_solution(3294939092410923446)
XLA Ops:
  0.6 91.3 %shard_map.110 = (bf16[512,768]{1,0:T(8,128)(2,1)}, bf16[512,768]{1,0:T(8,128)(2,1)}, f32[96,4096]{1,0:T(8,128)}, f32[8,128]{1,0:T(8,128)}, f32[16,128]{1,0:T(8,128)}) custom-call(bf16[128,4096]{1,0:T(8,128)(2,1)} %tok_hbm.1, s32[8,128]{1,0:T(8,128)} %bitcast.12, f32[8,128]{1,0:T(8,128)} %bitcast.13, bf16[512,768]{1,0:T(8,128)(2,1)} %bitcast.10, ...), custom_call_target="tpu_custom_call" | custom-call | tf_op jit(solution)/shard_map/pallas_call | solution.py:553
  91.9 3.2 %shard_map.111 = (bf16[512,768]{1,0:T(8,128)(2,1)}, bf16[512,768]{1,0:T(8,128)(2,1)}, f32[96,4096]{1,0:T(8,128)}, f32[8,128]{1,0:T(8,128)}, f32[16,128]{1,0:T(8,128)}) custom-call(bf16[512,768]{1,0:T(8,128)(2,1)} %get-tuple-element.15.refs_0_, bf16[512,768]{1,0:T(8,128)(2,1)} %get-tuple-element.16.refs_1_, f32[96,4096]{1,0:T(8,128)} %get-tuple-element.17.refs_2_, ...), custom_call_target="tpu_custom_call" | custom-call | tf_op jit(solution)/shard_map/pallas_call | solution.py:597

commit v6 on v5

--- a/solution.py
+++ b/solution.py
@@ -237,8 +237,7 @@
             cols = pl.ds(c * DC + q * 256, 256)
             block = dot(hw_t[...], recv[:, cols]).astype(BF)
             term[:, :, :, cols] = block.reshape(4, 2, OWN, 256)
-        cols = pl.ds(c * DC, DC)
-        send(term.at[:, 1 - core, :, cols], pair.at[:, :, cols], p_s, p_r.at[c], sibling)
+            send(term.at[:, 1 - core, :, cols], pair.at[:, :, cols], p_s, p_r.at[c], sibling)
 
     def make_hidden(c):
         if c == 1:
@@ -267,15 +266,16 @@
         cols = pl.ds(c * DC, DC)
         drain(pair.at[:, :, cols], p_r.at[c])
 
-        def one(k, carry):
-            both = term[k, core, :, cols].astype(F32) + pair[k, :, cols].astype(F32)
-            psum[k, :, cols] = both.astype(BF)
-            return carry
-
-        lax.fori_loop(0, 4, one, 0)
+        def add(block):
+            both = term[block, core, :, cols].astype(F32) + pair[block, :, cols].astype(F32)
+            psum[block, :, cols] = both.astype(BF)
+
         for way, part, target, sign in ways(c):
             block = (zhi + 4 - sign) % 4
+            add(block)
             send(psum.at[block, :, part], ring.at[0, :, part], g_s, g_r.at[c, 0, way], target)
+        add((zhi + 2) % 4)
+        add(zhi)
 
     def ring_step(c, step):
         for way, part, target, sign in ways(c):

time: 95.3 us -> 97.7 us (1.025)
  Pallas kernels: 94.5 us -> 96.9 us
    pallas_call x1, Pallas kernels: 91.3 us -> 93.7 us  [per_device(): pl.pallas_call(body, out_shape=(jax.ShapeDtypeStruct((SLOTS, FFE), BF), j...]
where the time goes in v6:
time: 97.7 us; the launch traced here: 97.6 us
  Pallas kernels  96.9 us (99%)
    pallas_call x1, Pallas kernels, per_device(): pl.pallas_call(body, out_shape=(jax.ShapeDtypeStruct((SLOTS, FFE), BF), j...  93.7 us
    pallas_call x1, Pallas kernels, hand_over(): pl.pallas_call(hand_over_body, out_shape=[jax.ShapeDtypeStruct(a.shape, a...  3.22 us

profile of v6, /device:TPU:1, one launch (start us, length us, event | category | flops | bytes accessed | tf_op | source)
XLA Modules:
  0.0 97.6 jit_solution(15090019675394492004)
XLA Ops:
  0.6 93.7 %shard_map.110 = (bf16[512,768]{1,0:T(8,128)(2,1)}, bf16[512,768]{1,0:T(8,128)(2,1)}, f32[96,4096]{1,0:T(8,128)}, f32[8,128]{1,0:T(8,128)}, f32[16,128]{1,0:T(8,128)}) custom-call(bf16[128,4096]{1,0:T(8,128)(2,1)} %tok_hbm.1, s32[8,128]{1,0:T(8,128)} %bitcast.12, f32[8,128]{1,0:T(8,128)} %bitcast.13, bf16[512,768]{1,0:T(8,128)(2,1)} %bitcast.10, ...), custom_call_target="tpu_custom_call" | custom-call | tf_op jit(solution)/shard_map/pallas_call | solution.py:553
  94.4 3.2 %shard_map.111 = (bf16[512,768]{1,0:T(8,128)(2,1)}, bf16[512,768]{1,0:T(8,128)(2,1)}, f32[96,4096]{1,0:T(8,128)}, f32[8,128]{1,0:T(8,128)}, f32[16,128]{1,0:T(8,128)}) custom-call(bf16[512,768]{1,0:T(8,128)(2,1)} %get-tuple-element.15.refs_0_, bf16[512,768]{1,0:T(8,128)(2,1)} %get-tuple-element.16.refs_1_, f32[96,4096]{1,0:T(8,128)} %get-tuple-element.17.refs_2_, ...), custom_call_target="tpu_custom_call" | custom-call | tf_op jit(solution)/shard_map/pallas_call | solution.py:597
